TPU v7x, 32 devices: a whole 2x2x4 slice. The times are simulated.
32 devices in a mesh: groups: 2 (over y), strip: 16 (over z, x, core).
Axes of the slice: x: 2, y: 2, z: 4, core: 2. Of those that a mesh axis runs over, the one named last changes fastest.
Arguments:
- data: bfloat16 [512, 128, 256], P(('groups', 'strip')), parts along dimension 0, may hold values from -6 to 6
- response: bfloat16 [256, 256], replicated
- pixel_ids: int32 [256], replicated, may hold values from 0 to 255, each once
- shift_bins: int32 [2, 256], replicated, may hold values from -64 to 64, as said below
Outputs:
- aligned: bfloat16 [256, 512, 128], P('strip', 'groups'), parts along dimension 1
- image_sum: float32 [512, 128], P(('groups', 'strip')), parts along dimension 0
- correlation: float32 [512, 81], P(('groups', 'strip')), parts along dimension 0
There are 2 independent parts, one for each index of `groups`. A program takes and returns all parts, laid end to end along the dimension named above; an argument that names none is the same for every part. Nothing has to cross between parts.
Inputs may be any that keep to these rules, and one draw needn't show every extreme that they name: `shift_bins`: every value in [-64, 64] may occur; both ends occur in each row.
All inputs are finite; a program needn't handle non-finite values.
Results may differ from a plain program's by a relative error of at most 0.0072.
Values may be sent and summed in bfloat16 or wider, within the bound.
A program may use at most 128 MiB of HBM per device.

v0:
```python
import math

import jax
import jax.numpy as jnp
from jax import lax
from jax.sharding import PartitionSpec as P

HALO = 16
LAGS = 4


def tap_weights(shift_bins):
    offsets = jnp.arange(-HALO, HALO + 1).astype(jnp.float32)
    shifted = offsets[None, None, :] - shift_bins[:, :, None].astype(jnp.float32) / 4.0
    kernel = jnp.sinc(shifted) * (0.5 + 0.5 * jnp.cos(jnp.pi * shifted / (HALO + 1)))
    return jnp.where(jnp.abs(shifted) < HALO + 1, kernel, 0.0).astype(jnp.bfloat16)


def make_bands(tap_table):
    out_rows = jnp.arange(HALO)[:, None]
    in_rows = jnp.arange(3 * HALO)[None, :]
    tap_index = out_rows + 2 * HALO - in_rows
    selector = (tap_index[:, :, None] == jnp.arange(2 * HALO + 1)[None, None, :]).astype(
        jnp.bfloat16
    )
    bands = jnp.einsum("yrj,ij->iyr", selector, tap_table, preferred_element_type=jnp.float32)
    return bands.astype(jnp.bfloat16)


def shift_rows(padded, bands):
    pix_count = padded.shape[0]
    row_count = padded.shape[1] - 2 * HALO
    col_count = padded.shape[2]
    blocks = row_count // HALO
    running = jnp.zeros((pix_count, blocks, HALO, col_count), jnp.float32)
    for third in range(3):
        section = padded[:, third * HALO : third * HALO + row_count].reshape(
            pix_count, blocks, HALO, col_count
        )
        band_part = bands[:, :, third * HALO : (third + 1) * HALO]
        running = running + jnp.einsum(
            "iyr,ibrx->ibyx", band_part, section, preferred_element_type=jnp.float32
        )
    return running.reshape(pix_count, row_count, col_count).astype(jnp.bfloat16)


def shift_columns(images, col_bands):
    pix_count, row_count, col_count = images.shape
    blocks = col_count // HALO
    padded = jnp.pad(images, ((0, 0), (0, 0), (HALO, HALO)))
    running = jnp.zeros((pix_count, row_count, blocks, HALO), jnp.float32)
    for third in range(3):
        section = padded[:, :, third * HALO : third * HALO + col_count].reshape(
            pix_count, row_count, blocks, HALO
        )
        band_part = col_bands[:, :, third * HALO : (third + 1) * HALO]
        running = running + jnp.einsum(
            "ixr,iybr->iybx", band_part, section, preferred_element_type=jnp.float32
        )
    return running.reshape(pix_count, row_count, col_count).astype(jnp.bfloat16)


def correlate(images, ref_pad):
    pix_count, row_count, col_count = images.shape
    wide_count = col_count + 2 * LAGS
    targets = jnp.arange(wide_count)[None, :, None]
    diag_table = (
        targets == jnp.arange(col_count)[:, None, None] + jnp.arange(2 * LAGS + 1)[None, None, :]
    ).astype(jnp.float32)
    columns = []
    for lag_row in range(2 * LAGS + 1):
        ref_rows = ref_pad[lag_row : lag_row + row_count]
        products = lax.dot_general(
            images, ref_rows, (((1,), (0,)), ((), ())), preferred_element_type=jnp.float32
        )
        columns.append(
            jnp.einsum("ixq,xqb->ib", products, diag_table, precision=lax.Precision.HIGHEST)
        )
    return jnp.concatenate(columns, axis=1)


def on_device(data, response, pixel_ids, shift_bins):
    row_count, col_count, pix_count = data.shape
    strip_count = lax.axis_size("strip")
    selection = (jnp.arange(pix_count)[:, None] == pixel_ids[None, :]).astype(jnp.bfloat16)
    chosen = jnp.dot(response, selection, preferred_element_type=jnp.float32).astype(jnp.bfloat16)
    corrected = lax.dot_general(
        chosen, data, (((0,), (2,)), ((), ())), preferred_element_type=jnp.float32
    ).astype(jnp.bfloat16)
    weights = tap_weights(shift_bins)
    bands = make_bands(weights[0])
    col_bands = make_bands(weights[1])
    pixel_part = lax.all_to_all(corrected, "strip", split_axis=0, concat_axis=1, tiled=True)
    part_count = pixel_part.shape[0]
    first_pixel = lax.axis_index("strip") * part_count
    band_part = lax.dynamic_slice_in_dim(bands, first_pixel, part_count, 0)
    col_part = lax.dynamic_slice_in_dim(col_bands, first_pixel, part_count, 0)
    padded = jnp.pad(pixel_part, ((0, 0), (HALO, HALO), (0, 0)))
    aligned = shift_columns(shift_rows(padded, band_part), col_part)
    image_sum = lax.psum_scatter(
        jnp.sum(aligned, axis=0, dtype=jnp.float32), "strip", scatter_dimension=0, tiled=True
    )
    whole_image = lax.all_gather(image_sum.astype(jnp.bfloat16), "strip", axis=0, tiled=True)
    correlation = correlate(aligned, jnp.pad(whole_image, LAGS))
    scaling = 1.0 / math.sqrt(pix_count * row_count * strip_count * col_count)
    return (aligned, image_sum, correlation * scaling)


def solution(mesh):
    placed = (P(("groups", "strip"), None, None), P(), P(), P())
    return jax.shard_map(
        on_device,
        mesh=mesh,
        in_specs=placed,
        out_specs=(
            P("strip", "groups", None),
            P(("groups", "strip"), None),
            P(("groups", "strip"), None),
        ),
        check_vma=False,
    )
```

profile of v0, /device:TPU:0, one launch (start us, length us, event | category | flops | bytes accessed | tf_op | source)
XLA Modules:
  0.0 164.3 jit_solution(2883986453506877579)
XLA Ops:
  7.2 0.0 copy-start
  7.2 1.2 copy-done
  8.4 1.5 convolution_convert_fusion
  10.0 1.6 %copy.95 = bf16[256,16,128]{2,1,0:T(8,128)(2,1)} copy(bf16[256,16,128]{2,0,1:T(8,128)(2,1)S(1)} %convolution_convert_fusion) | data formatting | bytes 2097152 | tf_op jit(solution)/shard_map/convert_element_type | solution.py:89
  11.6 0.0 copy-start.1
  11.6 7.5 %all-to-all-start = ((bf16[256,16,128]{2,1,0:T(8,128)(2,1)}), bf16[256,16,128]{2,1,0:T(8,128)(2,1)S(1)}, u32[]{:S(2)}, u32[]{:S(2)}) async-start(bf16[256,16,128]{2,1,0:T(8,128)(2,1)} %copy.95), calls=%async_computation | async-start | bytes 2097152 | tf_op jit(solution)/shard_map/all_to_all | solution.py:93
  19.1 0.0 reduce-scatter.4.cloned.1.call-start
  19.2 0.0 copy-done.1
  19.2 0.1 iota_subtract_fusion
  19.3 0.5 fusion.97
  19.7 0.5 fusion.60
  20.2 0.5 fusion.59
  20.7 0.1 slice_bitcast_fusion.2
  20.8 0.1 slice_bitcast_fusion
  20.9 21.1 %all-to-all-done = bf16[256,16,128]{2,1,0:T(8,128)(2,1)S(1)} async-done(((bf16[256,16,128]{2,1,0:T(8,128)(2,1)}), bf16[256,16,128]{2,1,0:T(8,128)(2,1)S(1)}, u32[]{:S(2)}, u32[]{:S(2)}) %all-to-all-start) | async-done | bytes 1048608 | tf_op jit(solution)/shard_map/all_to_all | solution.py:93
  42.0 0.3 copy.96
  42.3 0.4 pad_slice_fusion.2
  42.7 0.4 fusion.48
  43.1 0.4 fusion.131
  43.5 0.4 add_convert_fusion.1
  43.9 1.9 %pad_slice_fusion = (bf16[16,256,128]{2,1,0:T(8,128)(2,1)}, bf16[16,256,128]{2,1,0:T(8,128)(2,1)}) fusion(bf16[16,256,128]{2,1,0:T(8,128)(2,1)S(1)} %bitcast.112), kind=kLoop, calls=%fused_computation.2 | loop fusion | bytes 3145728 | tf_op jit(solution)/shard_map/slice | solution.py:53
  45.9 1.5 copy.104
  47.4 2.3 %copy.100 = bf16[16,256,128]{1,2,0:T(8,128)(2,1)} copy(bf16[16,256,128]{2,1,0:T(8,128)(2,1)} %get-tuple-element.19) | data formatting | bytes 2097152 | tf_op jit(solution)/shard_map/slice | solution.py:53
  49.6 7.4 %convert_element_type.80 = bf16[16,256,8,16]{3,2,1,0:T(8,128)(2,1)} reshape(bf16[16,16,16,128]{3,2,1,0:T(8,128)(2,1)S(1)} %bitcast.113) | data formatting | bytes 2097152 | tf_op jit(solution)/shard_map/convert_element_type | solution.py:44
  57.0 1.6 fusion.127
  58.6 5.6 %fusion = f32[16,256,8,16]{1,3,2,0:T(8,128)S(1)} fusion(bf16[16,256,8,16]{3,2,1,0:T(8,128)(2,1)} %convert_element_type.80, bf16[16,16,16,1]{2,0,1,3:T(8,128)(2,1)S(1)} %get-tuple-element.23), kind=kOutput, calls=%fused_computation | convolution fusion | flops 16777216 | bytes 3153920 | tf_op jit(solution)/shard_map/ixr,iybr->iybx/dot_general | solution.py:57
  64.3 0.5 convert_reduce_fusion
  64.7 0.8 copy.155
  65.5 0.0 reduce-scatter.4.cloned.1.call-update
  65.5 1.3 copy.126
  66.8 56.1 %reduce-scatter.4.cloned.1.call-done = f32[16,128]{1,0:T(8,128)} async-done(((f32[256,128]{1,0:T(8,128)}), f32[16,128]{1,0:T(8,128)}) %reduce-scatter.4.cloned.1.call-update) | async-done | bytes 8208
  123.0 0.7 convert_element_type.84
  123.7 19.7 %all_gather.3 = bf16[256,128]{1,0:T(8,128)(2,1)S(1)} all-gather(bf16[16,128]{1,0:T(8,128)(2,1)S(1)} %convert_element_type.84), channel_id=1, replica_groups=mesh['groups'=2,'strip'=16] {'strip'}, dimensions={0}, use_global_device_ids=true | all-gather | bytes 69632 | tf_op jit(solution)/shard_map/all_gather | solution.py:103
  143.4 0.1 copy.107
  143.5 0.5 fusion.99
  144.0 0.5 fusion.102
  144.5 0.5 fusion.105
  144.9 0.5 fusion.108
  145.4 0.5 fusion.111
  145.9 0.5 fusion.114
  146.4 0.5 fusion.117
  146.9 0.5 fusion.120
  147.4 0.5 fusion.123
  147.8 1.0 fusion.21
  148.8 1.0 fusion.24
  149.8 1.0 fusion.27
  150.8 1.0 fusion.30
  151.8 1.0 fusion.33
  152.8 1.0 fusion.36
  153.8 1.0 fusion.39
  154.8 1.0 fusion.42
  155.7 1.0 fusion.45
  156.7 0.1 concatenate.3
  156.8 0.6 broadcast_multiply_fusion
  (5 shorter events, 0.0 us)
Async XLA Ops:
  7.2 1.2 copy-start
  11.6 7.6 %copy-start.1 = (s32[2,256]{1,0:T(2,128)S(1)}, s32[2,256]{1,0:T(2,128)}, u32[]{:S(2)}) copy-start(s32[2,256]{1,0:T(2,128)} %param.7) | copy-start | bytes 6148
  11.6 30.4 %all-to-all-start = ((bf16[256,16,128]{2,1,0:T(8,128)(2,1)}), bf16[256,16,128]{2,1,0:T(8,128)(2,1)S(1)}, u32[]{:S(2)}, u32[]{:S(2)}) async-start(bf16[256,16,128]{2,1,0:T(8,128)(2,1)} %copy.95), calls=%async_computation | async-start | bytes 2097152 | tf_op jit(solution)/shard_map/all_to_all | solution.py:93
  19.1 103.9 %reduce-scatter.4.cloned.1.call-start = ((), (), s32[]{:S(2)}) async-start(), calls=%async_computation.2 | async-start | bytes 139264
Sparse Core Ops, SparseCore 0:
  65.6 57.2 reduce-scatter.3
where the time goes:
time: 165 us; the launch traced here: 164 us
  waiting for transfers between devices  77.3 us (47%)
  matrix products  24.7 us (15%)
  blocking collectives  19.7 us (12%)
  local copies, waits for them, and re-layouts  19.1 us (12%)
  between operations  14.2 us (9%)
  starting transfers between devices  7.53 us (5%)
  other arithmetic  1.86 us (1%)
    unnamed x2, waiting for transfers between devices  56.1 us
    all_to_all x1, waiting for transfers between devices, on_device(): lax.all_to_all(corrected, 'strip', split_axis=0, concat_axis=1, tiled=True)  21.1 us
    all_gather x1, blocking collectives, on_device(): lax.all_gather(image_sum.astype(jnp.bfloat16), 'strip', axis=0, tiled=True)  19.7 us
    dot_general x9, matrix products, correlate(): jnp.einsum('ixq,xqb->ib', products, diag_table, precision=lax.Precision.H...  8.88 us
    dot_general x3, matrix products, shift_columns(): jnp.einsum('ixr,iybr->iybx', band_part, section, preferred_element_type=j...  7.75 us
    all_to_all x1, starting transfers between devices, on_device(): lax.all_to_all(corrected, 'strip', split_axis=0, concat_axis=1, tiled=True)  7.49 us
    convert_element_type x1, local copies, waits for them, and re-layouts, shift_rows(): return running.reshape(pix_count, row_count, col_count).astype(jnp.bfloat16)  7.35 us
    slice x3, local copies, waits for them, and re-layouts, shift_columns(): padded[:, :, third * HALO:third * HALO + col_count]  5.68 us
  transfers between devices with their start and end apart: 2, of which 2 were waited for; matrix products, arithmetic and copies ran while one was open for 2% of the time, Pallas kernels for 0%

commit v1 on v0

v1 whole, which is shorter than its diff:
```python
import functools
import math

import jax
import jax.numpy as jnp
from jax import lax
from jax.experimental import pallas as pl
from jax.experimental.pallas import tpu as pltpu
from jax.sharding import PartitionSpec as P

HALO = 16
LAGS = 4
TAPS = 2 * HALO + 1
WIDE = 2 * LAGS + 1
SUB = 8
MESH = pl.DeviceIdType.MESH


def tap_value(offset, bins):
    u = offset.astype(jnp.float32) - bins.astype(jnp.float32) / 4.0
    angle = jnp.pi * u
    safe = jnp.where(u == 0.0, 1.0, angle)
    sinc = jnp.where(u == 0.0, 1.0, jnp.sin(safe) / safe)
    value = sinc * (0.5 + 0.5 * jnp.cos(angle / (HALO + 1)))
    inside = (jnp.abs(u) < HALO + 1) & (jnp.abs(offset) <= HALO)
    return jnp.where(inside, value, 0.0).astype(jnp.bfloat16)


def kernel(
    n, chunks, scaling,
    data_ref, resp_ref, ids_ref, bins_ref, bins_smem,
    aligned_ref, sum_ref, corr_out_ref,
    spread, natural, corrected, received, row_bands, col_bands,
    row_table, row_taps, col_taps, totals, halo_out, halo_in, image, image_pad, image_t, diagonals,
    send_sems, recv_sems, halo_send, halo_recv, image_send, image_recv, own_sem,
):
    rows, cols, pixels = data_ref.shape
    part = pixels // n
    size = part // chunks
    height = n * rows
    block = min(128, height)
    reach = rows + 2 * HALO
    me = lax.axis_index("strip")

    barrier = pltpu.get_barrier_semaphore()

    def greet(t, carry):
        other = lax.rem(me + t, n)
        pl.semaphore_signal(barrier, inc=1, device_id={"strip": other}, device_id_type=MESH)
        return carry

    lax.fori_loop(1, n, greet, 0)

    pick = lax.broadcasted_iota(jnp.int32, (pixels, pixels), 0) == ids_ref[...]
    chosen = jnp.dot(
        resp_ref[...], pick.astype(jnp.float32).astype(jnp.bfloat16), preferred_element_type=jnp.float32
    )
    chosen_t = chosen.T.astype(jnp.bfloat16)
    for y in range(rows):
        row = lax.dot_general(
            chosen_t, data_ref[y], (((1,), (1,)), ((), ())), preferred_element_type=jnp.float32
        )
        natural[y] = row.astype(jnp.bfloat16)
        spread[pl.ds(y, pixels, stride=rows), :] = row
    corrected[...] = spread[...].reshape(pixels, rows, cols).astype(jnp.bfloat16)

    pl.semaphore_wait(barrier, n - 1)

    def strip_copy(chunk, other, owner, sender):
        return pltpu.make_async_remote_copy(
            src_ref=corrected.at[pl.ds(owner * part + chunk * size, size)],
            dst_ref=received.at[
                pl.ds(chunk * size, size), pl.ds(pl.multiple_of(HALO + sender * rows, HALO), rows)
            ],
            send_sem=send_sems.at[chunk, other],
            recv_sem=recv_sems.at[chunk, sender],
            device_id={"strip": other},
            device_id_type=MESH,
        )

    def partner(step):
        half = lax.div(step + 1, 2)
        far = n // 2 + jnp.where(lax.rem(step, 2) == 0, half, -half)
        return lax.rem(me + far, n)

    def send_chunk(chunk):
        def one(step, carry):
            other = partner(step)
            strip_copy(chunk, other, other, me).start()
            return carry

        lax.fori_loop(0, n - 1, one, 0)

    first_sent = (chunks + 1) // 2
    for chunk in range(first_sent):
        send_chunk(chunk)
    own_copy = pltpu.make_async_copy(
        corrected.at[pl.ds(me * part, part)],
        received.at[:, pl.ds(pl.multiple_of(HALO + me * rows, HALO), rows)],
        own_sem,
    )
    own_copy.start()

    taps_at = lax.broadcasted_iota(jnp.int32, (reach + rows, pixels), 0)
    row_table[...] = tap_value(taps_at - (rows - 1) - HALO, bins_ref[0:1, :]).astype(jnp.float32)
    for y in range(rows):
        row_taps[y] = row_table[pl.ds(rows - 1 - y, reach), :].astype(jnp.bfloat16)
    for j in range(TAPS):
        offset = jnp.full((1, pixels), j - HALO, jnp.int32)
        tap = tap_value(offset, bins_ref[1:2, :]).astype(jnp.float32)
        col_taps[j] = jnp.broadcast_to(tap, (16, pixels)).astype(jnp.bfloat16)
    totals[...] = jnp.zeros_like(totals)

    def add_row(y, carry):
        taps = row_taps[y].reshape(1, reach // 16, 16, pixels)
        outer = (taps * col_taps[...].reshape(TAPS, 1, 16, pixels)).reshape(TAPS * reach, pixels)
        totals[...] += jnp.dot(outer, natural[y], preferred_element_type=jnp.float32)
        return carry

    lax.fori_loop(0, rows, add_row, 0)
    lane = lax.broadcasted_iota(jnp.int32, (reach, cols), 1)
    share = jnp.zeros((reach, cols), jnp.float32)
    for j in range(TAPS):
        shift = j - HALO
        moved = totals[pl.ds(j * reach, reach), :]
        if shift:
            moved = pltpu.roll(moved, shift % cols, 1)
            source = lane - shift
            moved = jnp.where((source >= 0) & (source < cols), moved, 0.0)
        share = share + moved
    halo_out[...] = share

    before, after = lax.rem(me + n - 1, n), lax.rem(me + 1, n)

    def halo_copy(side, other, start):
        return pltpu.make_async_remote_copy(
            src_ref=halo_out.at[pl.ds(start, HALO)],
            dst_ref=halo_in.at[side],
            send_sem=halo_send.at[side],
            recv_sem=halo_recv.at[side],
            device_id={"strip": other},
            device_id_type=MESH,
        )

    to_after = halo_copy(0, after, HALO + rows)
    to_before = halo_copy(1, before, 0)
    to_after.start()
    to_before.start()
    for chunk in range(first_sent, chunks):
        if chunk == chunks - 1:
            break
        send_chunk(chunk)
    to_after.wait_recv()
    to_before.wait_recv()
    mine = halo_out[pl.ds(HALO, rows), :]
    fill = jnp.zeros((rows - HALO, cols), jnp.float32)
    from_before = jnp.where(me > 0, halo_in[0], 0.0)
    from_after = jnp.where(me < n - 1, halo_in[1], 0.0)
    if rows > HALO:
        from_before = jnp.concatenate([from_before, fill], axis=0)
        from_after = jnp.concatenate([fill, from_after], axis=0)
    mine = mine + from_before + from_after
    sum_ref[...] = mine
    image[pl.ds(pl.multiple_of(me * rows, HALO), rows), :] = mine.astype(jnp.bfloat16)

    def image_copy(other, sender):
        place = pl.ds(pl.multiple_of(sender * rows, HALO), rows)
        return pltpu.make_async_remote_copy(
            src_ref=image.at[place],
            dst_ref=image.at[place],
            send_sem=image_send.at[other],
            recv_sem=image_recv.at[sender],
            device_id={"strip": other},
            device_id_type=MESH,
        )

    def send_image(step, carry):
        image_copy(partner(step), me).start()
        return carry

    lax.fori_loop(0, n - 1, send_image, 0)
    if chunks > first_sent:
        send_chunk(chunks - 1)

    band_lane = lax.broadcasted_iota(jnp.int32, (1, 2 * block), 1)
    col_lane = lax.broadcasted_iota(jnp.int32, (1, cols), 1)
    col_offset = jnp.where(col_lane < cols // 2, col_lane, col_lane - cols)
    square = (cols, cols)
    near = (
        jnp.abs(lax.broadcasted_iota(jnp.int32, square, 0) - lax.broadcasted_iota(jnp.int32, square, 1))
        <= HALO
    )

    def bands(i, carry):
        pixel = me * part + i
        row_line = tap_value(HALO - band_lane, bins_smem[0, pixel]).astype(jnp.float32)
        row_band = jnp.broadcast_to(row_line, (block, 2 * block))
        row_bands[i] = pltpu.roll(row_band, 0, 1, stride=1, stride_axis=0).astype(jnp.bfloat16)
        col_line = tap_value(col_offset, bins_smem[1, pixel]).astype(jnp.float32)
        col_band = jnp.broadcast_to(col_line, square)
        col_band = pltpu.roll(col_band, 0, 1, stride=1, stride_axis=0)
        col_bands[i] = jnp.where(near, col_band, 0.0).astype(jnp.bfloat16)
        return carry

    lax.fori_loop(0, part, bands, 0)
    edge = jnp.zeros((part, HALO, cols), jnp.bfloat16)
    received[:, pl.ds(0, HALO), :] = edge
    received[:, pl.ds(HALO + height, HALO), :] = edge

    def await_image(step, carry):
        other = lax.rem(me + step, n)
        image_copy(other, other).wait_recv()
        return carry

    lax.fori_loop(1, n, await_image, 0)
    image_pad[pl.ds(0, SUB), :] = jnp.zeros((SUB, cols), jnp.float32)
    image_pad[pl.ds(SUB + height, SUB), :] = jnp.zeros((SUB, cols), jnp.float32)
    image_pad[pl.ds(SUB, height), :] = image[...].astype(jnp.float32)
    for a in range(WIDE):
        window = image_pad[pl.ds(SUB + a - LAGS, height), :]
        image_t[pl.ds(a * cols, cols), :] = window.T.astype(jnp.bfloat16)

    own_copy.wait()
    low_lane = lax.broadcasted_iota(jnp.int32, (SUB, cols), 1) < cols // 2
    tail_lane = lax.broadcasted_iota(jnp.int32, (SUB, cols), 1)
    tail_keep = (tail_lane < SUB) | (tail_lane >= cols // 2)
    pieces = cols // SUB

    def work_chunk(chunk, carry):
        def await_strip(step, inner):
            other = lax.rem(me + step, n)
            strip_copy(chunk, other, other, other).wait_recv()
            return inner

        lax.fori_loop(1, n, await_strip, 0)

        def pair(index, inner):
            first = chunk * size + 2 * index
            images = []
            for k in range(2):
                i = first + k
                row_band = row_bands[i][:, : block + 2 * HALO]
                col_band = col_bands[i]
                parts = []
                for start in range(0, height, block):
                    window = received[i, pl.ds(start, block + 2 * HALO), :]
                    moved = jnp.dot(row_band, window, preferred_element_type=jnp.float32)
                    moved = jnp.dot(
                        moved.astype(jnp.bfloat16), col_band, preferred_element_type=jnp.float32
                    ).astype(jnp.bfloat16)
                    aligned_ref[i, pl.ds(start, block), :] = moved
                    parts.append(moved)
                images.append(jnp.concatenate(parts, axis=0))
            both = jnp.concatenate(images, axis=1)
            for a in range(WIDE):
                products = jnp.dot(
                    image_t[pl.ds(a * cols, cols), :], both, preferred_element_type=jnp.float32
                )
                for k in range(2):
                    total = None
                    for piece in range(pieces):
                        term = products[piece * SUB : (piece + 1) * SUB, k * cols : (k + 1) * cols]
                        if piece:
                            term = pltpu.roll(term, cols - piece * SUB, 1)
                        if piece == 0:
                            term = jnp.where(low_lane, term, 0.0)
                        elif piece == pieces - 1:
                            term = jnp.where(tail_keep, term, 0.0)
                        total = term if total is None else total + term
                    place = pl.multiple_of((a * part + first + k) * SUB, SUB)
                    diagonals[pl.ds(place, SUB), :] = total
            return inner

        lax.fori_loop(0, size // 2, pair, 0)
        return carry

    lax.fori_loop(0, chunks, work_chunk, 0)

    gathered = jnp.zeros((WIDE * part, cols), jnp.float32)
    lane_in = lax.broadcasted_iota(jnp.int32, square, 0)
    lane_out = lax.broadcasted_iota(jnp.int32, square, 1)
    for s in range(SUB):
        wanted = s - (lane_out - LAGS)
        wanted = jnp.where(wanted < 0, wanted + cols, wanted)
        choose = ((lane_in == wanted) & (lane_out < WIDE)).astype(jnp.float32)
        gathered = gathered + jnp.dot(
            diagonals[pl.ds(s, WIDE * part, stride=SUB), :],
            choose,
            precision=lax.Precision.HIGHEST,
            preferred_element_type=jnp.float32,
        )
    result = jnp.zeros((part, cols), jnp.float32)
    for a in range(WIDE):
        lags = gathered[a * part : (a + 1) * part, :]
        result = result + (pltpu.roll(lags, a * WIDE, 1) if a else lags)
    corr_out_ref[...] = (result * scaling)[:, : WIDE * WIDE]

    def drain(step, carry):
        other = lax.rem(me + step, n)
        for chunk in range(chunks):
            strip_copy(chunk, other, other, me).wait_send()
        image_copy(other, me).wait_send()
        return carry

    lax.fori_loop(1, n, drain, 0)
    to_after.wait_send()
    to_before.wait_send()


def on_device(data, response, pixel_ids, shift_bins):
    rows, cols, pixels = data.shape
    n = lax.axis_size("strip")
    part = pixels // n
    chunks = max(1, part // 4)
    height = n * rows
    block = min(128, height)
    reach = rows + 2 * HALO
    assert rows >= HALO and (part // chunks) % 2 == 0 and height % block == 0
    scaling = 1.0 / math.sqrt(pixels * height * cols)
    vmem = pl.BlockSpec(memory_space=pltpu.VMEM)
    bf16, f32 = jnp.bfloat16, jnp.float32
    return pl.pallas_call(
        functools.partial(kernel, n, chunks, scaling),
        out_shape=(
            jax.ShapeDtypeStruct((part, height, cols), bf16),
            jax.ShapeDtypeStruct((rows, cols), f32),
            jax.ShapeDtypeStruct((part, WIDE * WIDE), f32),
        ),
        in_specs=[vmem] * 4 + [pl.BlockSpec(memory_space=pltpu.SMEM)],
        out_specs=(vmem, vmem, vmem),
        scratch_shapes=[
            pltpu.VMEM((pixels * rows, cols), f32),
            pltpu.VMEM((rows, pixels, cols), bf16),
            pltpu.VMEM((pixels, rows, cols), bf16),
            pltpu.VMEM((part, height + 2 * HALO, cols), bf16),
            pltpu.VMEM((part, block, 2 * block), bf16),
            pltpu.VMEM((part, cols, cols), bf16),
            pltpu.VMEM((reach + rows, pixels), f32),
            pltpu.VMEM((rows, reach, pixels), bf16),
            pltpu.VMEM((TAPS, 16, pixels), bf16),
            pltpu.VMEM((TAPS * reach, cols), f32),
            pltpu.VMEM((reach, cols), f32),
            pltpu.VMEM((2, HALO, cols), f32),
            pltpu.VMEM((height, cols), bf16),
            pltpu.VMEM((height + 2 * SUB, cols), f32),
            pltpu.VMEM((WIDE * cols, height), bf16),
            pltpu.VMEM((WIDE * part * SUB, cols), f32),
            pltpu.SemaphoreType.DMA((chunks, n)),
            pltpu.SemaphoreType.DMA((chunks, n)),
            pltpu.SemaphoreType.DMA((2,)),
            pltpu.SemaphoreType.DMA((2,)),
            pltpu.SemaphoreType.DMA((n,)),
            pltpu.SemaphoreType.DMA((n,)),
            pltpu.SemaphoreType.DMA(()),
        ],
        compiler_params=pltpu.CompilerParams(
            collective_id=0, has_side_effects=True, vmem_limit_bytes=48 * 1024 * 1024
        ),
    )(data, response, pixel_ids.reshape(1, pixels), shift_bins, shift_bins)


def solution(mesh):
    placed = (P(("groups", "strip"), None, None), P(), P(), P())
    return jax.shard_map(
        on_device,
        mesh=mesh,
        in_specs=placed,
        out_specs=(
            P("strip", "groups", None),
            P(("groups", "strip"), None),
            P(("groups", "strip"), None),
        ),
        check_vma=False,
    )
```

time: 165 us -> 48.5 us (0.29)
  waiting for transfers between devices: 77.3 us -> 0 us
  Pallas kernels: 0 us -> 42 us
  matrix products: 24.7 us -> 0 us
  blocking collectives: 19.7 us -> 0 us
  between operations: 14.2 us -> 0.65 us
  local copies, waits for them, and re-layouts: 19.1 us -> 5.65 us
  starting transfers between devices: 7.53 us -> 0 us
  other arithmetic: 1.86 us -> 0 us
    unnamed x2 -> x0, waiting for transfers between devices: 56.1 us -> none
    pallas_call x0 -> x1, Pallas kernels: none -> 42 us  [on_device(): pl.pallas_call(functools.partial(kernel, n, chunks, scaling), out_shape=(...]
    dot_general x27 -> x0, matrix products: 24.7 us -> none  [the longest x9 8.88 us: correlate(): jnp.einsum('ixq,xqb->ib', products, diag_table, precision=lax.Precision.H...]
    all_to_all x1 -> x0, waiting for transfers between devices: 21.1 us -> none  [on_device(): lax.all_to_all(corrected, 'strip', split_axis=0, concat_axis=1, tiled=True)]
    all_gather x1 -> x0, blocking collectives: 19.7 us -> none  [on_device(): lax.all_gather(image_sum.astype(jnp.bfloat16), 'strip', axis=0, tiled=True)]
    convert_element_type x3 -> x0, local copies, waits for them, and re-layouts: 9.03 us -> none  [the longest x1 7.35 us: shift_rows(): return running.reshape(pix_count, row_count, col_count).astype(jnp.bfloat16)]
    all_to_all x1 -> x0, starting transfers between devices: 7.49 us -> none  [on_device(): lax.all_to_all(corrected, 'strip', split_axis=0, concat_axis=1, tiled=True)]
    slice x6 -> x0, local copies, waits for them, and re-layouts: 6.27 us -> none  [the longest x3 5.68 us: shift_columns(): padded[:, :, third * HALO:third * HALO + col_count]]
  transfers between devices with their start and end apart: 2 -> 0, of which waited for: 2 -> 0; matrix products, arithmetic and copies ran while one was open for 2% -> 0% of each run, Pallas kernels for 0% -> 0%
where the time goes in v1:
time: 48.5 us; the launch traced here: 48.3 us
  Pallas kernels  42 us (87%)
  local copies, waits for them, and re-layouts  5.65 us (12%)
  between operations  0.65 us (1%)
    pallas_call x1, Pallas kernels, on_device(): pl.pallas_call(functools.partial(kernel, n, chunks, scaling), out_shape=(...  42 us
    unnamed x11, local copies, waits for them, and re-layouts  5.65 us

profile of v1, /device:TPU:0, one launch (start us, length us, event | category | flops | bytes accessed | tf_op | source)
XLA Modules:
  0.0 48.3 jit_solution(15414060768826354935)
XLA Ops:
  0.6 0.0 copy-start.3
  0.6 0.7 %copy-done.3 = s32[256]{0:T(256)S(1)} copy-done((s32[256]{0:T(256)S(1)}, s32[256]{0:T(256)}, u32[]{:S(2)}) %copy-start.3) | copy-done | bytes 1048
  1.3 0.0 copy-start
  1.3 1.2 %copy-done = bf16[16,128,256]{2,1,0:T(8,128)(2,1)S(1)} copy-done((bf16[16,128,256]{2,1,0:T(8,128)(2,1)S(1)}, bf16[16,128,256]{2,1,0:T(8,128)(2,1)}, u32[]{:S(2)}) %copy-start) | copy-done | bytes 1048600
  2.5 0.0 copy-start.1
  2.5 0.9 %copy-done.1 = bf16[256,256]{1,0:T(8,128)(2,1)S(1)} copy-done((bf16[256,256]{1,0:T(8,128)(2,1)S(1)}, bf16[256,256]{1,0:T(8,128)(2,1)}, u32[]{:S(2)}) %copy-start.1) | copy-done | bytes 131096
  3.4 0.0 copy-start.2
  3.4 0.7 %copy-done.2 = s32[2,256]{1,0:T(2,128)S(1)} copy-done((s32[2,256]{1,0:T(2,128)S(1)}, s32[2,256]{1,0:T(2,128)}, u32[]{:S(2)}) %copy-start.2) | copy-done | bytes 2072
  4.1 42.0 %shard_map.67 = (bf16[16,256,128]{2,1,0:T(8,128)(2,1)S(1)}, f32[16,128]{1,0:T(8,128)S(1)}, f32[16,81]{1,0:T(8,128)S(1)}) custom-call(bf16[16,128,256]{2,1,0:T(8,128)(2,1)S(1)} %copy-done, bf16[256,256]{1,0:T(8,128)(2,1)S(1)} %copy-done.1, s32[1,256]{1,0:T(1,128)S(1)} %bitcast.1, s32[2,256]{1,0:T(2,128)S(1)} %copy-done.2, s32[2,256]{1,0:T(2,128)S(1)} %copy-done.2), custom_call_target="tpu_custom_call" | custom-call | tf_op jit(solution)/shard_map/pallas_call | solution.py:322
  46.1 1.0 %copy.10 = bf16[16,256,128]{2,1,0:T(8,128)(2,1)} copy(bf16[16,256,128]{2,1,0:T(8,128)(2,1)S(1)} %get-tuple-element.6) | data formatting | bytes 2097152
  47.1 0.6 %copy.11 = f32[16,128]{1,0:T(8,128)} copy(f32[16,128]{1,0:T(8,128)S(1)} %get-tuple-element.7) | data formatting | bytes 16384
  47.7 0.6 %copy.12 = f32[16,81]{1,0:T(8,128)} copy(f32[16,81]{1,0:T(8,128)S(1)} %get-tuple-element.8) | data formatting | bytes 10368
Async XLA Ops:
  0.6 0.7 %copy-start.3 = (s32[256]{0:T(256)S(1)}, s32[256]{0:T(256)}, u32[]{:S(2)}) copy-start(s32[256]{0:T(256)} %param.6) | copy-start | bytes 3076
  1.3 1.2 %copy-start = (bf16[16,128,256]{2,1,0:T(8,128)(2,1)S(1)}, bf16[16,128,256]{2,1,0:T(8,128)(2,1)}, u32[]{:S(2)}) copy-start(bf16[16,128,256]{2,1,0:T(8,128)(2,1)} %data_ref.1) | copy-start | bytes 3145732
  2.5 0.9 %copy-start.1 = (bf16[256,256]{1,0:T(8,128)(2,1)S(1)}, bf16[256,256]{1,0:T(8,128)(2,1)}, u32[]{:S(2)}) copy-start(bf16[256,256]{1,0:T(8,128)(2,1)} %resp_ref.1) | copy-start | bytes 393220
  3.4 0.7 %copy-start.2 = (s32[2,256]{1,0:T(2,128)S(1)}, s32[2,256]{1,0:T(2,128)}, u32[]{:S(2)}) copy-start(s32[2,256]{1,0:T(2,128)} %bins_smem.1) | copy-start | bytes 6148

commit v2 on v1

--- a/solution.py
+++ b/solution.py
@@ -28,19 +28,38 @@
 
 def kernel(
     n, chunks, scaling,
-    data_ref, resp_ref, ids_ref, bins_ref, bins_smem,
-    aligned_ref, sum_ref, corr_out_ref,
-    spread, natural, corrected, received, row_bands, col_bands,
-    row_table, row_taps, col_taps, totals, halo_out, halo_in, image, image_pad, image_t, diagonals,
-    send_sems, recv_sems, halo_send, halo_recv, image_send, image_recv, own_sem,
+    data_hbm, resp_hbm, ids_hbm, bins_hbm,
+    aligned_hbm, sum_hbm, corr_hbm,
+    aligned_ref, sum_ref, corr_out_ref, data_ref, resp_ref, ids_ref, bins_ref, bins_smem,
+    spread, natural, corrected, received, row_bands, col_bands, row_bins, col_bins,
+    row_lines, col_lines, row_taps, col_taps,
+    totals, halo_out, halo_in, image, image_pad, image_t, diagonals,
+    send_sems, recv_sems, halo_send, halo_recv, image_send, image_recv, own_sem, load_sems, store_sems,
 ):
     rows, cols, pixels = data_ref.shape
+    half_rows = rows // 2
     part = pixels // n
     size = part // chunks
     height = n * rows
     block = min(128, height)
     reach = rows + 2 * HALO
+    span = TAPS + (-TAPS) % SUB
     me = lax.axis_index("strip")
+
+    loads = [
+        pltpu.make_async_copy(source, target, load_sems.at[k])
+        for k, (source, target) in enumerate(
+            (
+                (resp_hbm, resp_ref),
+                (ids_hbm, ids_ref),
+                (data_hbm, data_ref),
+                (bins_hbm, bins_ref),
+                (bins_hbm, bins_smem),
+            )
+        )
+    ]
+    for load in loads:
+        load.start()
 
     barrier = pltpu.get_barrier_semaphore()
 
@@ -51,17 +70,22 @@
 
     lax.fori_loop(1, n, greet, 0)
 
+    loads[0].wait()
+    loads[1].wait()
     pick = lax.broadcasted_iota(jnp.int32, (pixels, pixels), 0) == ids_ref[...]
     chosen = jnp.dot(
         resp_ref[...], pick.astype(jnp.float32).astype(jnp.bfloat16), preferred_element_type=jnp.float32
     )
     chosen_t = chosen.T.astype(jnp.bfloat16)
-    for y in range(rows):
-        row = lax.dot_general(
-            chosen_t, data_ref[y], (((1,), (1,)), ((), ())), preferred_element_type=jnp.float32
-        )
-        natural[y] = row.astype(jnp.bfloat16)
-        spread[pl.ds(y, pixels, stride=rows), :] = row
+    loads[2].wait()
+    for y in range(half_rows):
+        both_rows = jnp.concatenate([data_ref[y], data_ref[y + half_rows]], axis=0)
+        pair_rows = lax.dot_general(
+            chosen_t, both_rows, (((1,), (1,)), ((), ())), preferred_element_type=jnp.float32
+        )
+        natural[y] = pair_rows.astype(jnp.bfloat16)
+        spread[pl.ds(y, pixels, stride=rows), :] = pair_rows[:, :cols]
+        spread[pl.ds(y + half_rows, pixels, stride=rows), :] = pair_rows[:, cols:]
     corrected[...] = spread[...].reshape(pixels, rows, cols).astype(jnp.bfloat16)
 
     pl.semaphore_wait(barrier, n - 1)
@@ -91,8 +115,7 @@
 
         lax.fori_loop(0, n - 1, one, 0)
 
-    first_sent = (chunks + 1) // 2
-    for chunk in range(first_sent):
+    for chunk in range(chunks):
         send_chunk(chunk)
     own_copy = pltpu.make_async_copy(
         corrected.at[pl.ds(me * part, part)],
@@ -101,28 +124,27 @@
     )
     own_copy.start()
 
-    taps_at = lax.broadcasted_iota(jnp.int32, (reach + rows, pixels), 0)
-    row_table[...] = tap_value(taps_at - (rows - 1) - HALO, bins_ref[0:1, :]).astype(jnp.float32)
-    for y in range(rows):
-        row_taps[y] = row_table[pl.ds(rows - 1 - y, reach), :].astype(jnp.bfloat16)
-    for j in range(TAPS):
-        offset = jnp.full((1, pixels), j - HALO, jnp.int32)
-        tap = tap_value(offset, bins_ref[1:2, :]).astype(jnp.float32)
-        col_taps[j] = jnp.broadcast_to(tap, (16, pixels)).astype(jnp.bfloat16)
+    loads[3].wait()
+    loads[4].wait()
+    taps_at = lax.broadcasted_iota(jnp.int32, (span, pixels), 0) - HALO
+    row_taps[...] = tap_value(taps_at, bins_ref[0:1, :]).astype(jnp.float32)
+    col_taps[...] = tap_value(taps_at, bins_ref[1:2, :]).astype(jnp.float32)
     totals[...] = jnp.zeros_like(totals)
-
-    def add_row(y, carry):
-        taps = row_taps[y].reshape(1, reach // 16, 16, pixels)
-        outer = (taps * col_taps[...].reshape(TAPS, 1, 16, pixels)).reshape(TAPS * reach, pixels)
-        totals[...] += jnp.dot(outer, natural[y], preferred_element_type=jnp.float32)
-        return carry
-
-    lax.fori_loop(0, rows, add_row, 0)
+    outer = row_taps[...].reshape(1, span, pixels) * col_taps[pl.ds(0, TAPS), :].reshape(TAPS, 1, pixels)
+    outer = outer.reshape(TAPS * span, pixels).astype(jnp.bfloat16)
+    gap = jnp.zeros((TAPS, half_rows, cols), jnp.float32)
+    for y in range(half_rows):
+        terms = jnp.dot(outer, natural[y], preferred_element_type=jnp.float32)
+        terms = terms.reshape(TAPS, span, 2 * cols)
+        terms = jnp.concatenate([terms[:, :, :cols], gap], axis=1) + jnp.concatenate(
+            [gap, terms[:, :, cols:]], axis=1
+        )
+        totals[:, pl.ds(y, span + half_rows), :] += terms
     lane = lax.broadcasted_iota(jnp.int32, (reach, cols), 1)
     share = jnp.zeros((reach, cols), jnp.float32)
     for j in range(TAPS):
         shift = j - HALO
-        moved = totals[pl.ds(j * reach, reach), :]
+        moved = totals[j, pl.ds(0, reach), :]
         if shift:
             moved = pltpu.roll(moved, shift % cols, 1)
             source = lane - shift
@@ -146,10 +168,33 @@
     to_before = halo_copy(1, before, 0)
     to_after.start()
     to_before.start()
-    for chunk in range(first_sent, chunks):
-        if chunk == chunks - 1:
-            break
-        send_chunk(chunk)
+    for i in range(part):
+        row_bins[pl.ds(i, 1), :] = jnp.full((1, 2 * block), bins_smem[0, me * part + i], jnp.int32)
+        col_bins[pl.ds(i, 1), :] = jnp.full((1, cols), bins_smem[1, me * part + i], jnp.int32)
+    band_lane = lax.broadcasted_iota(jnp.int32, (part, 2 * block), 1)
+    col_lane = lax.broadcasted_iota(jnp.int32, (part, cols), 1)
+    col_offset = jnp.where(col_lane < cols // 2, col_lane, col_lane - cols)
+    row_lines[...] = tap_value(HALO - band_lane, row_bins[...]).astype(jnp.float32)
+    col_lines[...] = tap_value(col_offset, col_bins[...]).astype(jnp.float32)
+    square = (cols, cols)
+    near = (
+        jnp.abs(lax.broadcasted_iota(jnp.int32, square, 0) - lax.broadcasted_iota(jnp.int32, square, 1))
+        <= HALO
+    )
+
+    def bands(i, carry):
+        row_band = jnp.broadcast_to(row_lines[pl.ds(i, 1), :], (block, 2 * block))
+        row_bands[i] = pltpu.roll(row_band, 0, 1, stride=1, stride_axis=0).astype(jnp.bfloat16)
+        col_band = jnp.broadcast_to(col_lines[pl.ds(i, 1), :], square)
+        col_band = pltpu.roll(col_band, 0, 1, stride=1, stride_axis=0)
+        col_bands[i] = jnp.where(near, col_band, 0.0).astype(jnp.bfloat16)
+        return carry
+
+    lax.fori_loop(0, part, bands, 0)
+    edge = jnp.zeros((part, HALO, cols), jnp.bfloat16)
+    received[:, pl.ds(0, HALO), :] = edge
+    received[:, pl.ds(HALO + height, HALO), :] = edge
+
     to_after.wait_recv()
     to_before.wait_recv()
     mine = halo_out[pl.ds(HALO, rows), :]
@@ -161,6 +206,8 @@
         from_after = jnp.concatenate([fill, from_after], axis=0)
     mine = mine + from_before + from_after
     sum_ref[...] = mine
+    sum_store = pltpu.make_async_copy(sum_ref, sum_hbm, store_sems.at[chunks])
+    sum_store.start()
     image[pl.ds(pl.multiple_of(me * rows, HALO), rows), :] = mine.astype(jnp.bfloat16)
 
     def image_copy(other, sender):
@@ -179,33 +226,37 @@
         return carry
 
     lax.fori_loop(0, n - 1, send_image, 0)
-    if chunks > first_sent:
-        send_chunk(chunks - 1)
-
-    band_lane = lax.broadcasted_iota(jnp.int32, (1, 2 * block), 1)
-    col_lane = lax.broadcasted_iota(jnp.int32, (1, cols), 1)
-    col_offset = jnp.where(col_lane < cols // 2, col_lane, col_lane - cols)
-    square = (cols, cols)
-    near = (
-        jnp.abs(lax.broadcasted_iota(jnp.int32, square, 0) - lax.broadcasted_iota(jnp.int32, square, 1))
-        <= HALO
-    )
-
-    def bands(i, carry):
-        pixel = me * part + i
-        row_line = tap_value(HALO - band_lane, bins_smem[0, pixel]).astype(jnp.float32)
-        row_band = jnp.broadcast_to(row_line, (block, 2 * block))
-        row_bands[i] = pltpu.roll(row_band, 0, 1, stride=1, stride_axis=0).astype(jnp.bfloat16)
-        col_line = tap_value(col_offset, bins_smem[1, pixel]).astype(jnp.float32)
-        col_band = jnp.broadcast_to(col_line, square)
-        col_band = pltpu.roll(col_band, 0, 1, stride=1, stride_axis=0)
-        col_bands[i] = jnp.where(near, col_band, 0.0).astype(jnp.bfloat16)
-        return carry
-
-    lax.fori_loop(0, part, bands, 0)
-    edge = jnp.zeros((part, HALO, cols), jnp.bfloat16)
-    received[:, pl.ds(0, HALO), :] = edge
-    received[:, pl.ds(HALO + height, HALO), :] = edge
+
+    def aligned_store(chunk):
+        place = pl.ds(chunk * size, size)
+        return pltpu.make_async_copy(aligned_ref.at[place], aligned_hbm.at[place], store_sems.at[chunk])
+
+    def align(chunk):
+        def await_strip(step, inner):
+            other = lax.rem(me + step, n)
+            strip_copy(chunk, other, other, other).wait_recv()
+            return inner
+
+        lax.fori_loop(1, n, await_strip, 0)
+
+        def one(index, inner):
+            i = chunk * size + index
+            row_band = row_bands[i][:, : block + 2 * HALO]
+            col_band = col_bands[i]
+            for start in range(0, height, block):
+                window = received[i, pl.ds(start, block + 2 * HALO), :]
+                moved = jnp.dot(row_band, window, preferred_element_type=jnp.float32)
+                moved = jnp.dot(
+                    moved.astype(jnp.bfloat16), col_band, preferred_element_type=jnp.float32
+                )
+                aligned_ref[i, pl.ds(start, block), :] = moved.astype(jnp.bfloat16)
+            return inner
+
+        lax.fori_loop(0, size, one, 0, unroll=True)
+        aligned_store(chunk).start()
+
+    own_copy.wait()
+    align(0)
 
     def await_image(step, carry):
         other = lax.rem(me + step, n)
@@ -220,38 +271,15 @@
         window = image_pad[pl.ds(SUB + a - LAGS, height), :]
         image_t[pl.ds(a * cols, cols), :] = window.T.astype(jnp.bfloat16)
 
-    own_copy.wait()
     low_lane = lax.broadcasted_iota(jnp.int32, (SUB, cols), 1) < cols // 2
     tail_lane = lax.broadcasted_iota(jnp.int32, (SUB, cols), 1)
     tail_keep = (tail_lane < SUB) | (tail_lane >= cols // 2)
     pieces = cols // SUB
 
-    def work_chunk(chunk, carry):
-        def await_strip(step, inner):
-            other = lax.rem(me + step, n)
-            strip_copy(chunk, other, other, other).wait_recv()
-            return inner
-
-        lax.fori_loop(1, n, await_strip, 0)
-
+    def correlate(chunk):
         def pair(index, inner):
             first = chunk * size + 2 * index
-            images = []
-            for k in range(2):
-                i = first + k
-                row_band = row_bands[i][:, : block + 2 * HALO]
-                col_band = col_bands[i]
-                parts = []
-                for start in range(0, height, block):
-                    window = received[i, pl.ds(start, block + 2 * HALO), :]
-                    moved = jnp.dot(row_band, window, preferred_element_type=jnp.float32)
-                    moved = jnp.dot(
-                        moved.astype(jnp.bfloat16), col_band, preferred_element_type=jnp.float32
-                    ).astype(jnp.bfloat16)
-                    aligned_ref[i, pl.ds(start, block), :] = moved
-                    parts.append(moved)
-                images.append(jnp.concatenate(parts, axis=0))
-            both = jnp.concatenate(images, axis=1)
+            both = jnp.concatenate([aligned_ref[first], aligned_ref[first + 1]], axis=1)
             for a in range(WIDE):
                 products = jnp.dot(
                     image_t[pl.ds(a * cols, cols), :], both, preferred_element_type=jnp.float32
@@ -272,9 +300,15 @@
             return inner
 
         lax.fori_loop(0, size // 2, pair, 0)
-        return carry
-
-    lax.fori_loop(0, chunks, work_chunk, 0)
+
+    correlate(0)
+
+    def work_chunk(chunk, carry):
+        align(chunk)
+        correlate(chunk)
+        return carry
+
+    lax.fori_loop(1, chunks, work_chunk, 0)
 
     gathered = jnp.zeros((WIDE * part, cols), jnp.float32)
     lane_in = lax.broadcasted_iota(jnp.int32, square, 0)
@@ -294,6 +328,8 @@
         lags = gathered[a * part : (a + 1) * part, :]
         result = result + (pltpu.roll(lags, a * WIDE, 1) if a else lags)
     corr_out_ref[...] = (result * scaling)[:, : WIDE * WIDE]
+    corr_store = pltpu.make_async_copy(corr_out_ref, corr_hbm, store_sems.at[chunks + 1])
+    corr_store.start()
 
     def drain(step, carry):
         other = lax.rem(me + step, n)
@@ -305,6 +341,18 @@
     lax.fori_loop(1, n, drain, 0)
     to_after.wait_send()
     to_before.wait_send()
+    for chunk in range(chunks):
+        aligned_store(chunk).wait()
+    sum_store.wait()
+    corr_store.wait()
+
+
+def write_out(*refs):
+    copies = [pltpu.make_async_copy(refs[k], refs[3 + k], refs[6].at[k]) for k in range(3)]
+    for copy in copies:
+        copy.start()
+    for copy in copies:
+        copy.wait()
 
 
 def on_device(data, response, pixel_ids, shift_bins):
@@ -315,30 +363,43 @@
     height = n * rows
     block = min(128, height)
     reach = rows + 2 * HALO
-    assert rows >= HALO and (part // chunks) % 2 == 0 and height % block == 0
+    assert rows >= HALO and rows % 16 == 0 and (part // chunks) % 2 == 0 and height % block == 0
     scaling = 1.0 / math.sqrt(pixels * height * cols)
-    vmem = pl.BlockSpec(memory_space=pltpu.VMEM)
+    span = TAPS + (-TAPS) % SUB
+    hbm = pl.BlockSpec(memory_space=pltpu.HBM)
     bf16, f32 = jnp.bfloat16, jnp.float32
-    return pl.pallas_call(
+    shapes = (
+        jax.ShapeDtypeStruct((part, height, cols), bf16),
+        jax.ShapeDtypeStruct((rows, cols), f32),
+        jax.ShapeDtypeStruct((part, WIDE * WIDE), f32),
+    )
+    results = pl.pallas_call(
         functools.partial(kernel, n, chunks, scaling),
-        out_shape=(
-            jax.ShapeDtypeStruct((part, height, cols), bf16),
-            jax.ShapeDtypeStruct((rows, cols), f32),
-            jax.ShapeDtypeStruct((part, WIDE * WIDE), f32),
-        ),
-        in_specs=[vmem] * 4 + [pl.BlockSpec(memory_space=pltpu.SMEM)],
-        out_specs=(vmem, vmem, vmem),
+        out_shape=shapes,
+        in_specs=[hbm] * 4,
+        out_specs=(hbm, hbm, hbm),
         scratch_shapes=[
+            pltpu.VMEM((part, height, cols), bf16),
+            pltpu.VMEM((rows, cols), f32),
+            pltpu.VMEM((part, WIDE * WIDE), f32),
+            pltpu.VMEM((rows, cols, pixels), bf16),
+            pltpu.VMEM((pixels, pixels), bf16),
+            pltpu.VMEM((1, pixels), jnp.int32),
+            pltpu.VMEM((2, pixels), jnp.int32),
+            pltpu.SMEM((2, pixels), jnp.int32),
             pltpu.VMEM((pixels * rows, cols), f32),
-            pltpu.VMEM((rows, pixels, cols), bf16),
+            pltpu.VMEM((rows // 2, pixels, 2 * cols), bf16),
             pltpu.VMEM((pixels, rows, cols), bf16),
             pltpu.VMEM((part, height + 2 * HALO, cols), bf16),
             pltpu.VMEM((part, block, 2 * block), bf16),
             pltpu.VMEM((part, cols, cols), bf16),
-            pltpu.VMEM((reach + rows, pixels), f32),
-            pltpu.VMEM((rows, reach, pixels), bf16),
-            pltpu.VMEM((TAPS, 16, pixels), bf16),
-            pltpu.VMEM((TAPS * reach, cols), f32),
+            pltpu.VMEM((part, 2 * block), jnp.int32),
+            pltpu.VMEM((part, cols), jnp.int32),
+            pltpu.VMEM((part, 2 * block), f32),
+            pltpu.VMEM((part, cols), f32),
+            pltpu.VMEM((span, pixels), f32),
+            pltpu.VMEM((span, pixels), f32),
+            pltpu.VMEM((TAPS, span + rows, cols), f32),
             pltpu.VMEM((reach, cols), f32),
             pltpu.VMEM((2, HALO, cols), f32),
             pltpu.VMEM((height, cols), bf16),
@@ -352,11 +413,21 @@
             pltpu.SemaphoreType.DMA((n,)),
             pltpu.SemaphoreType.DMA((n,)),
             pltpu.SemaphoreType.DMA(()),
+            pltpu.SemaphoreType.DMA((5,)),
+            pltpu.SemaphoreType.DMA((chunks + 2,)),
         ],
         compiler_params=pltpu.CompilerParams(
-            collective_id=0, has_side_effects=True, vmem_limit_bytes=48 * 1024 * 1024
+            collective_id=0, has_side_effects=True, vmem_limit_bytes=56 * 1024 * 1024
         ),
-    )(data, response, pixel_ids.reshape(1, pixels), shift_bins, shift_bins)
+    )(data, response, pixel_ids.reshape(1, pixels), shift_bins)
+    return pl.pallas_call(
+        write_out,
+        out_shape=shapes,
+        in_specs=[hbm] * 3,
+        out_specs=(hbm, hbm, hbm),
+        scratch_shapes=[pltpu.SemaphoreType.DMA((3,))],
+        compiler_params=pltpu.CompilerParams(vmem_limit_bytes=56 * 1024 * 1024),
+    )(*results)
 
 
 def solution(mesh):

time: 48.5 us -> 78.9 us (1.63)
  Pallas kernels: 42 us -> 78.1 us
  local copies, waits for them, and re-layouts: 5.65 us -> 0 us
    pallas_call x1 -> x2, Pallas kernels: 42 us -> 78.1 us  [the longest x1 44.7 us: on_device(): pl.pallas_call(functools.partial(kernel, n, chunks, scaling), out_shape=s...]
    unnamed x11 -> x0, local copies, waits for them, and re-layouts: 5.65 us -> none
where the time goes in v2:
time: 78.9 us; the launch traced here: 78.7 us
  Pallas kernels  78.1 us (99%)
    pallas_call x1, Pallas kernels, on_device(): pl.pallas_call(functools.partial(kernel, n, chunks, scaling), out_shape=s...  44.7 us
    pallas_call x1, Pallas kernels, on_device(): pl.pallas_call(write_out, out_shape=shapes, in_specs=[hbm] * 3, out_specs...  33.4 us

profile of v2, /device:TPU:0, one launch (start us, length us, event | category | flops | bytes accessed | tf_op | source)
XLA Modules:
  0.0 78.7 jit_solution(2907500498129445963)
XLA Ops:
  0.6 44.7 %shard_map.67 = (bf16[16,256,128]{2,1,0:T(8,128)(2,1)}, f32[16,128]{1,0:T(8,128)}, f32[16,81]{1,0:T(8,128)}) custom-call(bf16[16,128,256]{2,1,0:T(8,128)(2,1)} %data_hbm.1, bf16[256,256]{1,0:T(8,128)(2,1)} %resp_hbm.1, s32[1,256]{1,0:T(1,128)} %bitcast.1, s32[2,256]{1,0:T(2,128)} %bins_hbm.1), custom_call_target="tpu_custom_call" | custom-call | tf_op jit(solution)/shard_map/pallas_call | solution.py:376
  45.3 33.4 %shard_map.68 = (bf16[16,256,128]{2,1,0:T(8,128)(2,1)}, f32[16,128]{1,0:T(8,128)}, f32[16,81]{1,0:T(8,128)}) custom-call(bf16[16,256,128]{2,1,0:T(8,128)(2,1)} %get-tuple-element.6.refs_0_, f32[16,128]{1,0:T(8,128)} %get-tuple-element.7.refs_1_, f32[16,81]{1,0:T(8,128)} %get-tuple-element.8.refs_2_), custom_call_target="tpu_custom_call" | custom-call | tf_op jit(solution)/shard_map/pallas_call | solution.py:423

commit v3 on v2

--- a/solution.py
+++ b/solution.py
@@ -29,12 +29,12 @@
 def kernel(
     n, chunks, scaling,
     data_hbm, resp_hbm, ids_hbm, bins_hbm,
-    aligned_hbm, sum_hbm, corr_hbm,
-    aligned_ref, sum_ref, corr_out_ref, data_ref, resp_ref, ids_ref, bins_ref, bins_smem,
+    aligned_ref, sum_ref, corr_out_ref,
+    data_ref, resp_ref, ids_ref, bins_ref, bins_smem,
     spread, natural, corrected, received, row_bands, col_bands, row_bins, col_bins,
     row_lines, col_lines, row_taps, col_taps,
     totals, halo_out, halo_in, image, image_pad, image_t, diagonals,
-    send_sems, recv_sems, halo_send, halo_recv, image_send, image_recv, own_sem, load_sems, store_sems,
+    send_sems, recv_sems, halo_send, halo_recv, image_send, image_recv, own_sem, load_sems,
 ):
     rows, cols, pixels = data_ref.shape
     half_rows = rows // 2
@@ -93,9 +93,7 @@
     def strip_copy(chunk, other, owner, sender):
         return pltpu.make_async_remote_copy(
             src_ref=corrected.at[pl.ds(owner * part + chunk * size, size)],
-            dst_ref=received.at[
-                pl.ds(chunk * size, size), pl.ds(pl.multiple_of(HALO + sender * rows, HALO), rows)
-            ],
+            dst_ref=received.at[chunk, sender + 1],
             send_sem=send_sems.at[chunk, other],
             recv_sem=recv_sems.at[chunk, sender],
             device_id={"strip": other},
@@ -104,8 +102,10 @@
 
     def partner(step):
         half = lax.div(step + 1, 2)
-        far = n // 2 + jnp.where(lax.rem(step, 2) == 0, half, -half)
-        return lax.rem(me + far, n)
+        even = lax.rem(step, 2) == 0
+        if n & (n - 1):
+            return lax.rem(me + n // 2 + jnp.where(even, half, -half), n)
+        return me ^ jnp.where(even, n // 2 + half, half)
 
     def send_chunk(chunk):
         def one(step, carry):
@@ -115,14 +115,27 @@
 
         lax.fori_loop(0, n - 1, one, 0)
 
-    for chunk in range(chunks):
+    def await_left(chunk):
+        def one(step, carry):
+            other = partner(step)
+            strip_copy(chunk, other, other, me).wait_send()
+            return carry
+
+        lax.fori_loop(0, n - 1, one, 0)
+
+    ahead = min(2, chunks)
+    for chunk in range(ahead):
         send_chunk(chunk)
-    own_copy = pltpu.make_async_copy(
-        corrected.at[pl.ds(me * part, part)],
-        received.at[:, pl.ds(pl.multiple_of(HALO + me * rows, HALO), rows)],
-        own_sem,
-    )
-    own_copy.start()
+    own_copies = [
+        pltpu.make_async_copy(
+            corrected.at[pl.ds(me * part + chunk * size, size)],
+            received.at[chunk, me + 1],
+            own_sem.at[chunk],
+        )
+        for chunk in range(chunks)
+    ]
+    for own_copy in own_copies:
+        own_copy.start()
 
     loads[3].wait()
     loads[4].wait()
@@ -191,9 +204,12 @@
         return carry
 
     lax.fori_loop(0, part, bands, 0)
-    edge = jnp.zeros((part, HALO, cols), jnp.bfloat16)
-    received[:, pl.ds(0, HALO), :] = edge
-    received[:, pl.ds(HALO + height, HALO), :] = edge
+    edge = jnp.zeros((chunks, size, rows, cols), jnp.bfloat16)
+    received[:, 0] = edge
+    received[:, n + 1] = edge
+    if chunks > 2:
+        await_left(0)
+        send_chunk(2)
 
     to_after.wait_recv()
     to_before.wait_recv()
@@ -206,8 +222,6 @@
         from_after = jnp.concatenate([fill, from_after], axis=0)
     mine = mine + from_before + from_after
     sum_ref[...] = mine
-    sum_store = pltpu.make_async_copy(sum_ref, sum_hbm, store_sems.at[chunks])
-    sum_store.start()
     image[pl.ds(pl.multiple_of(me * rows, HALO), rows), :] = mine.astype(jnp.bfloat16)
 
     def image_copy(other, sender):
@@ -227,10 +241,6 @@
 
     lax.fori_loop(0, n - 1, send_image, 0)
 
-    def aligned_store(chunk):
-        place = pl.ds(chunk * size, size)
-        return pltpu.make_async_copy(aligned_ref.at[place], aligned_hbm.at[place], store_sems.at[chunk])
-
     def align(chunk):
         def await_strip(step, inner):
             other = lax.rem(me + step, n)
@@ -244,7 +254,8 @@
             row_band = row_bands[i][:, : block + 2 * HALO]
             col_band = col_bands[i]
             for start in range(0, height, block):
-                window = received[i, pl.ds(start, block + 2 * HALO), :]
+                window = received[chunk, pl.ds(start // rows, block // rows + 2), index]
+                window = window.reshape(block + 2 * rows, cols)[rows - HALO : rows + block + HALO]
                 moved = jnp.dot(row_band, window, preferred_element_type=jnp.float32)
                 moved = jnp.dot(
                     moved.astype(jnp.bfloat16), col_band, preferred_element_type=jnp.float32
@@ -253,9 +264,9 @@
             return inner
 
         lax.fori_loop(0, size, one, 0, unroll=True)
-        aligned_store(chunk).start()
-
-    own_copy.wait()
+
+    for own_copy in own_copies:
+        own_copy.wait()
     align(0)
 
     def await_image(step, carry):
@@ -271,6 +282,9 @@
         window = image_pad[pl.ds(SUB + a - LAGS, height), :]
         image_t[pl.ds(a * cols, cols), :] = window.T.astype(jnp.bfloat16)
 
+    for chunk in range(3, chunks):
+        await_left(chunk - 2)
+        send_chunk(chunk)
     low_lane = lax.broadcasted_iota(jnp.int32, (SUB, cols), 1) < cols // 2
     tail_lane = lax.broadcasted_iota(jnp.int32, (SUB, cols), 1)
     tail_keep = (tail_lane < SUB) | (tail_lane >= cols // 2)
@@ -311,40 +325,31 @@
     lax.fori_loop(1, chunks, work_chunk, 0)
 
     gathered = jnp.zeros((WIDE * part, cols), jnp.float32)
+    for s in range(SUB):
+        lines = diagonals[pl.ds(s, WIDE * part, stride=SUB), :]
+        turn = (LAGS - s) % cols
+        gathered = gathered + (pltpu.roll(lines, turn, 1) if turn else lines)
     lane_in = lax.broadcasted_iota(jnp.int32, square, 0)
     lane_out = lax.broadcasted_iota(jnp.int32, square, 1)
-    for s in range(SUB):
-        wanted = s - (lane_out - LAGS)
-        wanted = jnp.where(wanted < 0, wanted + cols, wanted)
-        choose = ((lane_in == wanted) & (lane_out < WIDE)).astype(jnp.float32)
-        gathered = gathered + jnp.dot(
-            diagonals[pl.ds(s, WIDE * part, stride=SUB), :],
-            choose,
-            precision=lax.Precision.HIGHEST,
-            preferred_element_type=jnp.float32,
-        )
+    mirror = ((lane_in + lane_out == 2 * LAGS) & (lane_out < WIDE)).astype(jnp.float32)
+    gathered = jnp.dot(
+        gathered, mirror, precision=lax.Precision.HIGHEST, preferred_element_type=jnp.float32
+    )
     result = jnp.zeros((part, cols), jnp.float32)
     for a in range(WIDE):
         lags = gathered[a * part : (a + 1) * part, :]
         result = result + (pltpu.roll(lags, a * WIDE, 1) if a else lags)
     corr_out_ref[...] = (result * scaling)[:, : WIDE * WIDE]
-    corr_store = pltpu.make_async_copy(corr_out_ref, corr_hbm, store_sems.at[chunks + 1])
-    corr_store.start()
 
     def drain(step, carry):
-        other = lax.rem(me + step, n)
-        for chunk in range(chunks):
-            strip_copy(chunk, other, other, me).wait_send()
-        image_copy(other, me).wait_send()
+        image_copy(lax.rem(me + step, n), me).wait_send()
         return carry
 
     lax.fori_loop(1, n, drain, 0)
+    for chunk in range(max(0, chunks - 2), chunks):
+        await_left(chunk)
     to_after.wait_send()
     to_before.wait_send()
-    for chunk in range(chunks):
-        aligned_store(chunk).wait()
-    sum_store.wait()
-    corr_store.wait()
 
 
 def write_out(*refs):
@@ -363,9 +368,10 @@
     height = n * rows
     block = min(128, height)
     reach = rows + 2 * HALO
-    assert rows >= HALO and rows % 16 == 0 and (part // chunks) % 2 == 0 and height % block == 0
+    assert rows >= HALO and rows % 16 == 0 and block % rows == 0 and (part // chunks) % 2 == 0 and height % block == 0
     scaling = 1.0 / math.sqrt(pixels * height * cols)
     span = TAPS + (-TAPS) % SUB
+    vmem = pl.BlockSpec(memory_space=pltpu.VMEM)
     hbm = pl.BlockSpec(memory_space=pltpu.HBM)
     bf16, f32 = jnp.bfloat16, jnp.float32
     shapes = (
@@ -377,11 +383,8 @@
         functools.partial(kernel, n, chunks, scaling),
         out_shape=shapes,
         in_specs=[hbm] * 4,
-        out_specs=(hbm, hbm, hbm),
+        out_specs=(vmem, vmem, vmem),
         scratch_shapes=[
-            pltpu.VMEM((part, height, cols), bf16),
-            pltpu.VMEM((rows, cols), f32),
-            pltpu.VMEM((part, WIDE * WIDE), f32),
             pltpu.VMEM((rows, cols, pixels), bf16),
             pltpu.VMEM((pixels, pixels), bf16),
             pltpu.VMEM((1, pixels), jnp.int32),
@@ -390,7 +393,7 @@
             pltpu.VMEM((pixels * rows, cols), f32),
             pltpu.VMEM((rows // 2, pixels, 2 * cols), bf16),
             pltpu.VMEM((pixels, rows, cols), bf16),
-            pltpu.VMEM((part, height + 2 * HALO, cols), bf16),
+            pltpu.VMEM((chunks, n + 2, part // chunks, rows, cols), bf16),
             pltpu.VMEM((part, block, 2 * block), bf16),
             pltpu.VMEM((part, cols, cols), bf16),
             pltpu.VMEM((part, 2 * block), jnp.int32),
@@ -412,21 +415,19 @@
             pltpu.SemaphoreType.DMA((2,)),
             pltpu.SemaphoreType.DMA((n,)),
             pltpu.SemaphoreType.DMA((n,)),
-            pltpu.SemaphoreType.DMA(()),
+            pltpu.SemaphoreType.DMA((chunks,)),
             pltpu.SemaphoreType.DMA((5,)),
-            pltpu.SemaphoreType.DMA((chunks + 2,)),
         ],
         compiler_params=pltpu.CompilerParams(
-            collective_id=0, has_side_effects=True, vmem_limit_bytes=56 * 1024 * 1024
+            collective_id=0, has_side_effects=True, vmem_limit_bytes=48 * 1024 * 1024
         ),
-    )(data, response, pixel_ids.reshape(1, pixels), shift_bins)
+    )(*(pltpu.with_memory_space_constraint(a, pltpu.HBM) for a in (data, response, pixel_ids.reshape(1, pixels), shift_bins)))
     return pl.pallas_call(
         write_out,
         out_shape=shapes,
-        in_specs=[hbm] * 3,
+        in_specs=[vmem] * 3,
         out_specs=(hbm, hbm, hbm),
         scratch_shapes=[pltpu.SemaphoreType.DMA((3,))],
-        compiler_params=pltpu.CompilerParams(vmem_limit_bytes=56 * 1024 * 1024),
     )(*results)
 
 

time: 78.9 us -> 44.2 us (0.56)
  Pallas kernels: 78.1 us -> 41.2 us
  local copies, waits for them, and re-layouts: 0 us -> 2.16 us
    pallas_call x1, Pallas kernels: 33.4 us -> 2.24 us  [on_device(): pl.pallas_call(write_out, out_shape=shapes, in_specs=[vmem] * 3, out_spec...]
    pallas_call x1, Pallas kernels: 44.7 us -> 38.9 us  [on_device(): pl.pallas_call(functools.partial(kernel, n, chunks, scaling), out_shape=s...]
    unnamed x0 -> x6, local copies, waits for them, and re-layouts: none -> 2.16 us
where the time goes in v3:
time: 44.2 us; the launch traced here: 44 us
  Pallas kernels  41.2 us (93%)
  local copies, waits for them, and re-layouts  2.16 us (5%)
  between operations  0.65 us (1%)
    pallas_call x1, Pallas kernels, on_device(): pl.pallas_call(functools.partial(kernel, n, chunks, scaling), out_shape=s...  38.9 us
    pallas_call x1, Pallas kernels, on_device(): pl.pallas_call(write_out, out_shape=shapes, in_specs=[vmem] * 3, out_spec...  2.24 us
    unnamed x6, local copies, waits for them, and re-layouts  2.16 us

profile of v3, /device:TPU:0, one launch (start us, length us, event | category | flops | bytes accessed | tf_op | source)
XLA Modules:
  0.0 44.0 jit_solution(16088301197320065314)
XLA Ops:
  0.6 38.9 %shard_map.67 = (bf16[16,256,128]{2,1,0:T(8,128)(2,1)S(1)}, f32[16,128]{1,0:T(8,128)S(1)}, f32[16,81]{1,0:T(8,128)S(1)}) custom-call(bf16[16,128,256]{2,1,0:T(8,128)(2,1)} %data_hbm.1, bf16[256,256]{1,0:T(8,128)(2,1)} %resp_hbm.1, s32[1,256]{1,0:T(1,128)} %bitcast.1, s32[2,256]{1,0:T(2,128)} %bins_hbm.1), custom_call_target="tpu_custom_call" | custom-call | tf_op jit(solution)/shard_map/pallas_call | solution.py:382
  39.6 0.0 copy-start
  39.6 1.0 %copy-done = bf16[16,256,128]{2,1,0:T(8,128)(2,1)} copy-done((bf16[16,256,128]{2,1,0:T(8,128)(2,1)}, bf16[16,256,128]{2,1,0:T(8,128)(2,1)S(1)}, u32[]{:S(2)}) %copy-start) | copy-done | bytes 1048600
  40.5 0.0 copy-start.1
  40.6 0.6 %copy-done.1 = f32[16,128]{1,0:T(8,128)} copy-done((f32[16,128]{1,0:T(8,128)}, f32[16,128]{1,0:T(8,128)S(1)}, u32[]{:S(2)}) %copy-start.1) | copy-done | bytes 8216
  41.2 0.0 copy-start.2
  41.2 0.6 %copy-done.2 = f32[16,81]{1,0:T(8,128)} copy-done((f32[16,81]{1,0:T(8,128)}, f32[16,81]{1,0:T(8,128)S(1)}, u32[]{:S(2)}) %copy-start.2) | copy-done | bytes 5208
  41.8 2.2 %shard_map.68 = (bf16[16,256,128]{2,1,0:T(8,128)(2,1)}, f32[16,128]{1,0:T(8,128)}, f32[16,81]{1,0:T(8,128)}) custom-call(bf16[16,256,128]{2,1,0:T(8,128)(2,1)} %copy-done, f32[16,128]{1,0:T(8,128)} %copy-done.1, f32[16,81]{1,0:T(8,128)} %copy-done.2), custom_call_target="tpu_custom_call" | custom-call | tf_op jit(solution)/shard_map/pallas_call | solution.py:425
Async XLA Ops:
  39.6 1.0 %copy-start = (bf16[16,256,128]{2,1,0:T(8,128)(2,1)}, bf16[16,256,128]{2,1,0:T(8,128)(2,1)S(1)}, u32[]{:S(2)}) copy-start(bf16[16,256,128]{2,1,0:T(8,128)(2,1)S(1)} %get-tuple-element.6.refs_0_) | copy-start | bytes 3145732
  40.5 0.6 %copy-start.1 = (f32[16,128]{1,0:T(8,128)}, f32[16,128]{1,0:T(8,128)S(1)}, u32[]{:S(2)}) copy-start(f32[16,128]{1,0:T(8,128)S(1)} %get-tuple-element.7.refs_1_) | copy-start | bytes 24580
  41.2 0.6 %copy-start.2 = (f32[16,81]{1,0:T(8,128)}, f32[16,81]{1,0:T(8,128)S(1)}, u32[]{:S(2)}) copy-start(f32[16,81]{1,0:T(8,128)S(1)} %get-tuple-element.8.refs_2_) | copy-start | bytes 15556

commit v4 on v3

--- a/solution.py
+++ b/solution.py
@@ -32,7 +32,7 @@
     aligned_ref, sum_ref, corr_out_ref,
     data_ref, resp_ref, ids_ref, bins_ref, bins_smem,
     spread, natural, corrected, received, row_bands, col_bands, row_bins, col_bins,
-    row_lines, col_lines, row_taps, col_taps,
+    row_lines, col_lines, row_taps, col_taps, outer_taps,
     totals, halo_out, halo_in, image, image_pad, image_t, diagonals,
     send_sems, recv_sems, halo_send, halo_recv, image_send, image_recv, own_sem, load_sems,
 ):
@@ -77,6 +77,14 @@
         resp_ref[...], pick.astype(jnp.float32).astype(jnp.bfloat16), preferred_element_type=jnp.float32
     )
     chosen_t = chosen.T.astype(jnp.bfloat16)
+    loads[3].wait()
+    loads[4].wait()
+    taps_at = lax.broadcasted_iota(jnp.int32, (span, pixels), 0) - HALO
+    row_taps[...] = tap_value(taps_at, bins_ref[0:1, :]).astype(jnp.float32)
+    col_taps[...] = tap_value(taps_at, bins_ref[1:2, :]).astype(jnp.float32)
+    totals[...] = jnp.zeros_like(totals)
+    outer = row_taps[...].reshape(1, span, pixels) * col_taps[pl.ds(0, TAPS), :].reshape(TAPS, 1, pixels)
+    outer_taps[...] = outer.reshape(TAPS * span, pixels).astype(jnp.bfloat16)
     loads[2].wait()
     for y in range(half_rows):
         both_rows = jnp.concatenate([data_ref[y], data_ref[y + half_rows]], axis=0)
@@ -123,9 +131,7 @@
 
         lax.fori_loop(0, n - 1, one, 0)
 
-    ahead = min(2, chunks)
-    for chunk in range(ahead):
-        send_chunk(chunk)
+    send_chunk(0)
     own_copies = [
         pltpu.make_async_copy(
             corrected.at[pl.ds(me * part + chunk * size, size)],
@@ -137,17 +143,9 @@
     for own_copy in own_copies:
         own_copy.start()
 
-    loads[3].wait()
-    loads[4].wait()
-    taps_at = lax.broadcasted_iota(jnp.int32, (span, pixels), 0) - HALO
-    row_taps[...] = tap_value(taps_at, bins_ref[0:1, :]).astype(jnp.float32)
-    col_taps[...] = tap_value(taps_at, bins_ref[1:2, :]).astype(jnp.float32)
-    totals[...] = jnp.zeros_like(totals)
-    outer = row_taps[...].reshape(1, span, pixels) * col_taps[pl.ds(0, TAPS), :].reshape(TAPS, 1, pixels)
-    outer = outer.reshape(TAPS * span, pixels).astype(jnp.bfloat16)
     gap = jnp.zeros((TAPS, half_rows, cols), jnp.float32)
     for y in range(half_rows):
-        terms = jnp.dot(outer, natural[y], preferred_element_type=jnp.float32)
+        terms = jnp.dot(outer_taps[...], natural[y], preferred_element_type=jnp.float32)
         terms = terms.reshape(TAPS, span, 2 * cols)
         terms = jnp.concatenate([terms[:, :, :cols], gap], axis=1) + jnp.concatenate(
             [gap, terms[:, :, cols:]], axis=1
@@ -181,6 +179,8 @@
     to_before = halo_copy(1, before, 0)
     to_after.start()
     to_before.start()
+    if chunks > 1:
+        send_chunk(1)
     for i in range(part):
         row_bins[pl.ds(i, 1), :] = jnp.full((1, 2 * block), bins_smem[0, me * part + i], jnp.int32)
         col_bins[pl.ds(i, 1), :] = jnp.full((1, cols), bins_smem[1, me * part + i], jnp.int32)
@@ -207,9 +207,6 @@
     edge = jnp.zeros((chunks, size, rows, cols), jnp.bfloat16)
     received[:, 0] = edge
     received[:, n + 1] = edge
-    if chunks > 2:
-        await_left(0)
-        send_chunk(2)
 
     to_after.wait_recv()
     to_before.wait_recv()
@@ -240,6 +237,8 @@
         return carry
 
     lax.fori_loop(0, n - 1, send_image, 0)
+    if chunks > 2:
+        send_chunk(2)
 
     def align(chunk):
         def await_strip(step, inner):
@@ -268,6 +267,9 @@
     for own_copy in own_copies:
         own_copy.wait()
     align(0)
+    for chunk in range(3, chunks):
+        await_left(chunk - 2)
+        send_chunk(chunk)
 
     def await_image(step, carry):
         other = lax.rem(me + step, n)
@@ -282,9 +284,6 @@
         window = image_pad[pl.ds(SUB + a - LAGS, height), :]
         image_t[pl.ds(a * cols, cols), :] = window.T.astype(jnp.bfloat16)
 
-    for chunk in range(3, chunks):
-        await_left(chunk - 2)
-        send_chunk(chunk)
     low_lane = lax.broadcasted_iota(jnp.int32, (SUB, cols), 1) < cols // 2
     tail_lane = lax.broadcasted_iota(jnp.int32, (SUB, cols), 1)
     tail_keep = (tail_lane < SUB) | (tail_lane >= cols // 2)
@@ -346,7 +345,7 @@
         return carry
 
     lax.fori_loop(1, n, drain, 0)
-    for chunk in range(max(0, chunks - 2), chunks):
+    for chunk in sorted({0, chunks - 1} | {min(c, chunks - 1) for c in (chunks - 2,) if c > 0}):
         await_left(chunk)
     to_after.wait_send()
     to_before.wait_send()
@@ -402,6 +401,7 @@
             pltpu.VMEM((part, cols), f32),
             pltpu.VMEM((span, pixels), f32),
             pltpu.VMEM((span, pixels), f32),
+            pltpu.VMEM((TAPS * span, pixels), bf16),
             pltpu.VMEM((TAPS, span + rows, cols), f32),
             pltpu.VMEM((reach, cols), f32),
             pltpu.VMEM((2, HALO, cols), f32),
@@ -428,6 +428,7 @@
         in_specs=[vmem] * 3,
         out_specs=(hbm, hbm, hbm),
         scratch_shapes=[pltpu.SemaphoreType.DMA((3,))],
+        compiler_params=pltpu.CompilerParams(vmem_limit_bytes=8 * 1024 * 1024),
     )(*results)
 
 

time: 44.2 us -> 39.5 us (0.89)
  Pallas kernels: 41.2 us -> 38.7 us
  local copies, waits for them, and re-layouts: 2.16 us -> 0 us
    unnamed x6 -> x0, local copies, waits for them, and re-layouts: 2.16 us -> none
    pallas_call x1, Pallas kernels: 38.9 us -> 37.7 us  [on_device(): pl.pallas_call(functools.partial(kernel, n, chunks, scaling), out_shape=s...]
    pallas_call x1, Pallas kernels: 2.24 us -> 1 us  [on_device(): pl.pallas_call(write_out, out_shape=shapes, in_specs=[vmem] * 3, out_spec...]
where the time goes in v4:
time: 39.5 us; the launch traced here: 39.3 us
  Pallas kernels  38.7 us (98%)
  between operations  0.64 us (2%)
    pallas_call x1, Pallas kernels, on_device(): pl.pallas_call(functools.partial(kernel, n, chunks, scaling), out_shape=s...  37.7 us
    pallas_call x1, Pallas kernels, on_device(): pl.pallas_call(write_out, out_shape=shapes, in_specs=[vmem] * 3, out_spec...  1 us

profile of v4, /device:TPU:0, one launch (start us, length us, event | category | flops | bytes accessed | tf_op | source)
XLA Modules:
  0.0 39.3 jit_solution(11989563527860560501)
XLA Ops:
  0.6 37.7 %shard_map.67 = (bf16[16,256,128]{2,1,0:T(8,128)(2,1)S(1)}, f32[16,128]{1,0:T(8,128)S(1)}, f32[16,81]{1,0:T(8,128)S(1)}) custom-call(bf16[16,128,256]{2,1,0:T(8,128)(2,1)} %data_hbm.1, bf16[256,256]{1,0:T(8,128)(2,1)} %resp_hbm.1, s32[1,256]{1,0:T(1,128)} %bitcast.1, s32[2,256]{1,0:T(2,128)} %bins_hbm.1), custom_call_target="tpu_custom_call" | custom-call | tf_op jit(solution)/shard_map/pallas_call | solution.py:381
  38.3 1.0 %shard_map.68 = (bf16[16,256,128]{2,1,0:T(8,128)(2,1)}, f32[16,128]{1,0:T(8,128)}, f32[16,81]{1,0:T(8,128)}) custom-call(bf16[16,256,128]{2,1,0:T(8,128)(2,1)S(1)} %get-tuple-element.6.refs_0_, f32[16,128]{1,0:T(8,128)S(1)} %get-tuple-element.7.refs_1_, f32[16,81]{1,0:T(8,128)S(1)} %get-tuple-element.8.refs_2_), custom_call_target="tpu_custom_call" | custom-call | tf_op jit(solution)/shard_map/pallas_call | solution.py:425

commit v5 on v3

--- a/solution.py
+++ b/solution.py
@@ -31,8 +31,8 @@
     data_hbm, resp_hbm, ids_hbm, bins_hbm,
     aligned_ref, sum_ref, corr_out_ref,
     data_ref, resp_ref, ids_ref, bins_ref, bins_smem,
-    spread, natural, corrected, received, row_bands, col_bands, row_bins, col_bins,
-    row_lines, col_lines, row_taps, col_taps,
+    chosen_t, spread, natural, corrected, received, row_bands, col_bands, row_bins, col_bins,
+    row_lines, col_lines, row_taps, col_taps, outer_taps,
     totals, halo_out, halo_in, image, image_pad, image_t, diagonals,
     send_sems, recv_sems, halo_send, halo_recv, image_send, image_recv, own_sem, load_sems,
 ):
@@ -76,19 +76,24 @@
     chosen = jnp.dot(
         resp_ref[...], pick.astype(jnp.float32).astype(jnp.bfloat16), preferred_element_type=jnp.float32
     )
-    chosen_t = chosen.T.astype(jnp.bfloat16)
+    chosen_t[...] = chosen.T.astype(jnp.bfloat16)
     loads[2].wait()
-    for y in range(half_rows):
-        both_rows = jnp.concatenate([data_ref[y], data_ref[y + half_rows]], axis=0)
-        pair_rows = lax.dot_general(
-            chosen_t, both_rows, (((1,), (1,)), ((), ())), preferred_element_type=jnp.float32
-        )
-        natural[y] = pair_rows.astype(jnp.bfloat16)
-        spread[pl.ds(y, pixels, stride=rows), :] = pair_rows[:, :cols]
-        spread[pl.ds(y + half_rows, pixels, stride=rows), :] = pair_rows[:, cols:]
-    corrected[...] = spread[...].reshape(pixels, rows, cols).astype(jnp.bfloat16)
-
-    pl.semaphore_wait(barrier, n - 1)
+
+    def correct(first, count):
+        first = pl.multiple_of(first, 16)
+        for y in range(half_rows):
+            both_rows = jnp.concatenate([data_ref[y], data_ref[y + half_rows]], axis=0)
+            pair_rows = lax.dot_general(
+                chosen_t[pl.ds(first, count), :],
+                both_rows,
+                (((1,), (1,)), ((), ())),
+                preferred_element_type=jnp.float32,
+            )
+            natural[y, pl.ds(first, count), :] = pair_rows.astype(jnp.bfloat16)
+            spread[pl.ds(first * rows + y, count, stride=rows), :] = pair_rows[:, :cols]
+            spread[pl.ds(first * rows + y + half_rows, count, stride=rows), :] = pair_rows[:, cols:]
+        flat = spread[pl.ds(pl.multiple_of(first * rows, 16), count * rows), :]
+        corrected[pl.ds(first, count)] = flat.reshape(count, rows, cols).astype(jnp.bfloat16)
 
     def strip_copy(chunk, other, owner, sender):
         return pltpu.make_async_remote_copy(
@@ -123,9 +128,32 @@
 
         lax.fori_loop(0, n - 1, one, 0)
 
-    ahead = min(2, chunks)
-    for chunk in range(ahead):
-        send_chunk(chunk)
+    early = min(2, chunks)
+    if n & (n - 1) or n < 4:
+        correct(0, pixels)
+        pl.semaphore_wait(barrier, n - 1)
+        for chunk in range(early):
+            send_chunk(chunk)
+    else:
+        side = lax.div(me, n // 2)
+        correct((1 - side) * (pixels // 2), pixels // 2)
+        pl.semaphore_wait(barrier, n - 1)
+
+        def send_far(step, carry):
+            other = me ^ (n // 2 + step)
+            strip_copy(0, other, other, me).start()
+            return carry
+
+        def send_near(step, carry):
+            other = me ^ step
+            strip_copy(0, other, other, me).start()
+            return carry
+
+        lax.fori_loop(0, n // 2, send_far, 0)
+        correct(side * (pixels // 2), pixels // 2)
+        lax.fori_loop(1, n // 2, send_near, 0)
+        for chunk in range(1, early):
+            send_chunk(chunk)
     own_copies = [
         pltpu.make_async_copy(
             corrected.at[pl.ds(me * part + chunk * size, size)],
@@ -144,10 +172,10 @@
     col_taps[...] = tap_value(taps_at, bins_ref[1:2, :]).astype(jnp.float32)
     totals[...] = jnp.zeros_like(totals)
     outer = row_taps[...].reshape(1, span, pixels) * col_taps[pl.ds(0, TAPS), :].reshape(TAPS, 1, pixels)
-    outer = outer.reshape(TAPS * span, pixels).astype(jnp.bfloat16)
+    outer_taps[...] = outer.reshape(TAPS * span, pixels).astype(jnp.bfloat16)
     gap = jnp.zeros((TAPS, half_rows, cols), jnp.float32)
     for y in range(half_rows):
-        terms = jnp.dot(outer, natural[y], preferred_element_type=jnp.float32)
+        terms = jnp.dot(outer_taps[...], natural[y], preferred_element_type=jnp.float32)
         terms = terms.reshape(TAPS, span, 2 * cols)
         terms = jnp.concatenate([terms[:, :, :cols], gap], axis=1) + jnp.concatenate(
             [gap, terms[:, :, cols:]], axis=1
@@ -181,6 +209,9 @@
     to_before = halo_copy(1, before, 0)
     to_after.start()
     to_before.start()
+    middle = min(4, chunks)
+    for chunk in range(early, middle):
+        send_chunk(chunk)
     for i in range(part):
         row_bins[pl.ds(i, 1), :] = jnp.full((1, 2 * block), bins_smem[0, me * part + i], jnp.int32)
         col_bins[pl.ds(i, 1), :] = jnp.full((1, cols), bins_smem[1, me * part + i], jnp.int32)
@@ -207,9 +238,6 @@
     edge = jnp.zeros((chunks, size, rows, cols), jnp.bfloat16)
     received[:, 0] = edge
     received[:, n + 1] = edge
-    if chunks > 2:
-        await_left(0)
-        send_chunk(2)
 
     to_after.wait_recv()
     to_before.wait_recv()
@@ -240,6 +268,8 @@
         return carry
 
     lax.fori_loop(0, n - 1, send_image, 0)
+    for chunk in range(middle, chunks):
+        send_chunk(chunk)
 
     def align(chunk):
         def await_strip(step, inner):
@@ -282,9 +312,6 @@
         window = image_pad[pl.ds(SUB + a - LAGS, height), :]
         image_t[pl.ds(a * cols, cols), :] = window.T.astype(jnp.bfloat16)
 
-    for chunk in range(3, chunks):
-        await_left(chunk - 2)
-        send_chunk(chunk)
     low_lane = lax.broadcasted_iota(jnp.int32, (SUB, cols), 1) < cols // 2
     tail_lane = lax.broadcasted_iota(jnp.int32, (SUB, cols), 1)
     tail_keep = (tail_lane < SUB) | (tail_lane >= cols // 2)
@@ -346,7 +373,7 @@
         return carry
 
     lax.fori_loop(1, n, drain, 0)
-    for chunk in range(max(0, chunks - 2), chunks):
+    for chunk in range(chunks):
         await_left(chunk)
     to_after.wait_send()
     to_before.wait_send()
@@ -364,7 +391,7 @@
     rows, cols, pixels = data.shape
     n = lax.axis_size("strip")
     part = pixels // n
-    chunks = max(1, part // 4)
+    chunks = max(1, part // 2)
     height = n * rows
     block = min(128, height)
     reach = rows + 2 * HALO
@@ -390,6 +417,7 @@
             pltpu.VMEM((1, pixels), jnp.int32),
             pltpu.VMEM((2, pixels), jnp.int32),
             pltpu.SMEM((2, pixels), jnp.int32),
+            pltpu.VMEM((pixels, pixels), bf16),
             pltpu.VMEM((pixels * rows, cols), f32),
             pltpu.VMEM((rows // 2, pixels, 2 * cols), bf16),
             pltpu.VMEM((pixels, rows, cols), bf16),
@@ -402,6 +430,7 @@
             pltpu.VMEM((part, cols), f32),
             pltpu.VMEM((span, pixels), f32),
             pltpu.VMEM((span, pixels), f32),
+            pltpu.VMEM((TAPS * span, pixels), bf16),
             pltpu.VMEM((TAPS, span + rows, cols), f32),
             pltpu.VMEM((reach, cols), f32),
             pltpu.VMEM((2, HALO, cols), f32),
@@ -428,6 +457,7 @@
         in_specs=[vmem] * 3,
         out_specs=(hbm, hbm, hbm),
         scratch_shapes=[pltpu.SemaphoreType.DMA((3,))],
+        compiler_params=pltpu.CompilerParams(vmem_limit_bytes=8 * 1024 * 1024),
     )(*results)
 
 

time: 44.2 us -> 42 us (0.950)
  local copies, waits for them, and re-layouts: 2.16 us -> 0 us
    unnamed x6 -> x0, local copies, waits for them, and re-layouts: 2.16 us -> none
    pallas_call x1, Pallas kernels: 38.9 us -> 40.2 us  [on_device(): pl.pallas_call(functools.partial(kernel, n, chunks, scaling), out_shape=s...]
    pallas_call x1, Pallas kernels: 2.24 us -> 1 us  [on_device(): pl.pallas_call(write_out, out_shape=shapes, in_specs=[vmem] * 3, out_spec...]
where the time goes in v5:
time: 42 us; the launch traced here: 41.9 us
  Pallas kernels  41.2 us (98%)
  between operations  0.64 us (2%)
    pallas_call x1, Pallas kernels, on_device(): pl.pallas_call(functools.partial(kernel, n, chunks, scaling), out_shape=s...  40.2 us
    pallas_call x1, Pallas kernels, on_device(): pl.pallas_call(write_out, out_shape=shapes, in_specs=[vmem] * 3, out_spec...  1 us

profile of v5, /device:TPU:0, one launch (start us, length us, event | category | flops | bytes accessed | tf_op | source)
XLA Modules:
  0.0 41.9 jit_solution(7039589964228097247)
XLA Ops:
  0.6 40.2 %shard_map.67 = (bf16[16,256,128]{2,1,0:T(8,128)(2,1)S(1)}, f32[16,128]{1,0:T(8,128)S(1)}, f32[16,81]{1,0:T(8,128)S(1)}) custom-call(bf16[16,128,256]{2,1,0:T(8,128)(2,1)} %data_hbm.1, bf16[256,256]{1,0:T(8,128)(2,1)} %resp_hbm.1, s32[1,256]{1,0:T(1,128)} %bitcast.1, s32[2,256]{1,0:T(2,128)} %bins_hbm.1), custom_call_target="tpu_custom_call" | custom-call | tf_op jit(solution)/shard_map/pallas_call | solution.py:409
  40.9 1.0 %shard_map.68 = (bf16[16,256,128]{2,1,0:T(8,128)(2,1)}, f32[16,128]{1,0:T(8,128)}, f32[16,81]{1,0:T(8,128)}) custom-call(bf16[16,256,128]{2,1,0:T(8,128)(2,1)S(1)} %get-tuple-element.6.refs_0_, f32[16,128]{1,0:T(8,128)S(1)} %get-tuple-element.7.refs_1_, f32[16,81]{1,0:T(8,128)S(1)} %get-tuple-element.8.refs_2_), custom_call_target="tpu_custom_call" | custom-call | tf_op jit(solution)/shard_map/pallas_call | solution.py:454

commit v6 on v5

--- a/solution.py
+++ b/solution.py
@@ -128,7 +128,7 @@
 
         lax.fori_loop(0, n - 1, one, 0)
 
-    early = min(2, chunks)
+    early = 1
     if n & (n - 1) or n < 4:
         correct(0, pixels)
         pl.semaphore_wait(barrier, n - 1)
@@ -209,7 +209,8 @@
     to_before = halo_copy(1, before, 0)
     to_after.start()
     to_before.start()
-    middle = min(4, chunks)
+    middle = min(2, chunks)
+    late = min(3, chunks)
     for chunk in range(early, middle):
         send_chunk(chunk)
     for i in range(part):
@@ -268,7 +269,7 @@
         return carry
 
     lax.fori_loop(0, n - 1, send_image, 0)
-    for chunk in range(middle, chunks):
+    for chunk in range(middle, late):
         send_chunk(chunk)
 
     def align(chunk):
@@ -298,6 +299,9 @@
     for own_copy in own_copies:
         own_copy.wait()
     align(0)
+    for chunk in range(late, chunks):
+        await_left(chunk - 2)
+        send_chunk(chunk)
 
     def await_image(step, carry):
         other = lax.rem(me + step, n)
@@ -374,7 +378,8 @@
 
     lax.fori_loop(1, n, drain, 0)
     for chunk in range(chunks):
-        await_left(chunk)
+        if not late - 2 <= chunk < chunks - 2 or chunks == late:
+            await_left(chunk)
     to_after.wait_send()
     to_before.wait_send()
 
@@ -391,7 +396,7 @@
     rows, cols, pixels = data.shape
     n = lax.axis_size("strip")
     part = pixels // n
-    chunks = max(1, part // 2)
+    chunks = max(1, part // 4)
     height = n * rows
     block = min(128, height)
     reach = rows + 2 * HALO

time: 42 us -> 38.3 us (0.912)
  Pallas kernels: 41.2 us -> 37.5 us
    pallas_call x1, Pallas kernels: 40.2 us -> 36.5 us  [on_device(): pl.pallas_call(functools.partial(kernel, n, chunks, scaling), out_shape=s...]
where the time goes in v6:
time: 38.3 us; the launch traced here: 38.1 us
  Pallas kernels  37.5 us (98%)
  between operations  0.64 us (2%)
    pallas_call x1, Pallas kernels, on_device(): pl.pallas_call(functools.partial(kernel, n, chunks, scaling), out_shape=s...  36.5 us
    pallas_call x1, Pallas kernels, on_device(): pl.pallas_call(write_out, out_shape=shapes, in_specs=[vmem] * 3, out_spec...  1 us

profile of v6, /device:TPU:0, one launch (start us, length us, event | category | flops | bytes accessed | tf_op | source)
XLA Modules:
  0.0 38.1 jit_solution(3816905014517758858)
XLA Ops:
  0.6 36.5 %shard_map.67 = (bf16[16,256,128]{2,1,0:T(8,128)(2,1)S(1)}, f32[16,128]{1,0:T(8,128)S(1)}, f32[16,81]{1,0:T(8,128)S(1)}) custom-call(bf16[16,128,256]{2,1,0:T(8,128)(2,1)} %data_hbm.1, bf16[256,256]{1,0:T(8,128)(2,1)} %resp_hbm.1, s32[1,256]{1,0:T(1,128)} %bitcast.1, s32[2,256]{1,0:T(2,128)} %bins_hbm.1), custom_call_target="tpu_custom_call" | custom-call | tf_op jit(solution)/shard_map/pallas_call | solution.py:414
  37.1 1.0 %shard_map.68 = (bf16[16,256,128]{2,1,0:T(8,128)(2,1)}, f32[16,128]{1,0:T(8,128)}, f32[16,81]{1,0:T(8,128)}) custom-call(bf16[16,256,128]{2,1,0:T(8,128)(2,1)S(1)} %get-tuple-element.6.refs_0_, f32[16,128]{1,0:T(8,128)S(1)} %get-tuple-element.7.refs_1_, f32[16,81]{1,0:T(8,128)S(1)} %get-tuple-element.8.refs_2_), custom_call_target="tpu_custom_call" | custom-call | tf_op jit(solution)/shard_map/pallas_call | solution.py:459

commit v7 on v6

--- a/solution.py
+++ b/solution.py
@@ -45,6 +45,7 @@
     reach = rows + 2 * HALO
     span = TAPS + (-TAPS) % SUB
     me = lax.axis_index("strip")
+    flat_loop = n <= 16
 
     loads = [
         pltpu.make_async_copy(source, target, load_sems.at[k])
@@ -68,7 +69,7 @@
         pl.semaphore_signal(barrier, inc=1, device_id={"strip": other}, device_id_type=MESH)
         return carry
 
-    lax.fori_loop(1, n, greet, 0)
+    lax.fori_loop(1, n, greet, 0, unroll=flat_loop)
 
     loads[0].wait()
     loads[1].wait()
@@ -118,7 +119,7 @@
             strip_copy(chunk, other, other, me).start()
             return carry
 
-        lax.fori_loop(0, n - 1, one, 0)
+        lax.fori_loop(0, n - 1, one, 0, unroll=flat_loop)
 
     def await_left(chunk):
         def one(step, carry):
@@ -126,7 +127,7 @@
             strip_copy(chunk, other, other, me).wait_send()
             return carry
 
-        lax.fori_loop(0, n - 1, one, 0)
+        lax.fori_loop(0, n - 1, one, 0, unroll=flat_loop)
 
     early = 1
     if n & (n - 1) or n < 4:
@@ -149,9 +150,9 @@
             strip_copy(0, other, other, me).start()
             return carry
 
-        lax.fori_loop(0, n // 2, send_far, 0)
+        lax.fori_loop(0, n // 2, send_far, 0, unroll=flat_loop)
         correct(side * (pixels // 2), pixels // 2)
-        lax.fori_loop(1, n // 2, send_near, 0)
+        lax.fori_loop(1, n // 2, send_near, 0, unroll=flat_loop)
         for chunk in range(1, early):
             send_chunk(chunk)
     own_copies = [
@@ -268,7 +269,7 @@
         image_copy(partner(step), me).start()
         return carry
 
-    lax.fori_loop(0, n - 1, send_image, 0)
+    lax.fori_loop(0, n - 1, send_image, 0, unroll=flat_loop)
     for chunk in range(middle, late):
         send_chunk(chunk)
 
@@ -278,7 +279,7 @@
             strip_copy(chunk, other, other, other).wait_recv()
             return inner
 
-        lax.fori_loop(1, n, await_strip, 0)
+        lax.fori_loop(1, n, await_strip, 0, unroll=flat_loop)
 
         def one(index, inner):
             i = chunk * size + index
@@ -308,7 +309,7 @@
         image_copy(other, other).wait_recv()
         return carry
 
-    lax.fori_loop(1, n, await_image, 0)
+    lax.fori_loop(1, n, await_image, 0, unroll=flat_loop)
     image_pad[pl.ds(0, SUB), :] = jnp.zeros((SUB, cols), jnp.float32)
     image_pad[pl.ds(SUB + height, SUB), :] = jnp.zeros((SUB, cols), jnp.float32)
     image_pad[pl.ds(SUB, height), :] = image[...].astype(jnp.float32)
@@ -348,12 +349,20 @@
 
     correlate(0)
 
-    def work_chunk(chunk, carry):
+    def drain(step, carry):
+        image_copy(lax.rem(me + step, n), me).wait_send()
+        return carry
+
+    lax.fori_loop(1, n, drain, 0, unroll=flat_loop)
+    to_after.wait_send()
+    to_before.wait_send()
+    left = set(range(late - 2, chunks - 2)) if chunks > late else set()
+    for chunk in range(1, chunks):
+        if chunk - 1 not in left:
+            await_left(chunk - 1)
+            left.add(chunk - 1)
         align(chunk)
         correlate(chunk)
-        return carry
-
-    lax.fori_loop(1, chunks, work_chunk, 0)
 
     gathered = jnp.zeros((WIDE * part, cols), jnp.float32)
     for s in range(SUB):
@@ -372,16 +381,8 @@
         result = result + (pltpu.roll(lags, a * WIDE, 1) if a else lags)
     corr_out_ref[...] = (result * scaling)[:, : WIDE * WIDE]
 
-    def drain(step, carry):
-        image_copy(lax.rem(me + step, n), me).wait_send()
-        return carry
-
-    lax.fori_loop(1, n, drain, 0)
-    for chunk in range(chunks):
-        if not late - 2 <= chunk < chunks - 2 or chunks == late:
-            await_left(chunk)
-    to_after.wait_send()
-    to_before.wait_send()
+    if chunks - 1 not in left:
+        await_left(chunks - 1)
 
 
 def write_out(*refs):

time: 38.3 us -> 37.4 us (0.977)
  Pallas kernels: 37.5 us -> 36.6 us
    pallas_call x1, Pallas kernels: 36.5 us -> 35.6 us  [on_device(): pl.pallas_call(functools.partial(kernel, n, chunks, scaling), out_shape=s...]
where the time goes in v7:
time: 37.4 us; the launch traced here: 37.3 us
  Pallas kernels  36.6 us (98%)
  between operations  0.64 us (2%)
    pallas_call x1, Pallas kernels, on_device(): pl.pallas_call(functools.partial(kernel, n, chunks, scaling), out_shape=s...  35.6 us
    pallas_call x1, Pallas kernels, on_device(): pl.pallas_call(write_out, out_shape=shapes, in_specs=[vmem] * 3, out_spec...  1 us

profile of v7, /device:TPU:0, one launch (start us, length us, event | category | flops | bytes accessed | tf_op | source)
XLA Modules:
  0.0 37.3 jit_solution(1544449755109014869)
XLA Ops:
  0.6 35.6 %shard_map.67 = (bf16[16,256,128]{2,1,0:T(8,128)(2,1)S(1)}, f32[16,128]{1,0:T(8,128)S(1)}, f32[16,81]{1,0:T(8,128)S(1)}) custom-call(bf16[16,128,256]{2,1,0:T(8,128)(2,1)} %data_hbm.1, bf16[256,256]{1,0:T(8,128)(2,1)} %resp_hbm.1, s32[1,256]{1,0:T(1,128)} %bitcast.1, s32[2,256]{1,0:T(2,128)} %bins_hbm.1), custom_call_target="tpu_custom_call" | custom-call | tf_op jit(solution)/shard_map/pallas_call | solution.py:415
  36.3 1.0 %shard_map.68 = (bf16[16,256,128]{2,1,0:T(8,128)(2,1)}, f32[16,128]{1,0:T(8,128)}, f32[16,81]{1,0:T(8,128)}) custom-call(bf16[16,256,128]{2,1,0:T(8,128)(2,1)S(1)} %get-tuple-element.6.refs_0_, f32[16,128]{1,0:T(8,128)S(1)} %get-tuple-element.7.refs_1_, f32[16,81]{1,0:T(8,128)S(1)} %get-tuple-element.8.refs_2_), custom_call_target="tpu_custom_call" | custom-call | tf_op jit(solution)/shard_map/pallas_call | solution.py:460

commit v8 on v7

--- a/solution.py
+++ b/solution.py
@@ -27,7 +27,7 @@
 
 
 def kernel(
-    n, chunks, scaling,
+    n, sizes, scaling,
     data_hbm, resp_hbm, ids_hbm, bins_hbm,
     aligned_ref, sum_ref, corr_out_ref,
     data_ref, resp_ref, ids_ref, bins_ref, bins_smem,
@@ -39,7 +39,8 @@
     rows, cols, pixels = data_ref.shape
     half_rows = rows // 2
     part = pixels // n
-    size = part // chunks
+    chunks = len(sizes)
+    firsts = [sum(sizes[:k]) for k in range(chunks)]
     height = n * rows
     block = min(128, height)
     reach = rows + 2 * HALO
@@ -98,8 +99,8 @@
 
     def strip_copy(chunk, other, owner, sender):
         return pltpu.make_async_remote_copy(
-            src_ref=corrected.at[pl.ds(owner * part + chunk * size, size)],
-            dst_ref=received.at[chunk, sender + 1],
+            src_ref=corrected.at[pl.ds(owner * part + firsts[chunk], sizes[chunk])],
+            dst_ref=received[chunk].at[sender + 1],
             send_sem=send_sems.at[chunk, other],
             recv_sem=recv_sems.at[chunk, sender],
             device_id={"strip": other},
@@ -157,8 +158,8 @@
             send_chunk(chunk)
     own_copies = [
         pltpu.make_async_copy(
-            corrected.at[pl.ds(me * part + chunk * size, size)],
-            received.at[chunk, me + 1],
+            corrected.at[pl.ds(me * part + firsts[chunk], sizes[chunk])],
+            received[chunk].at[me + 1],
             own_sem.at[chunk],
         )
         for chunk in range(chunks)
@@ -237,9 +238,10 @@
         return carry
 
     lax.fori_loop(0, part, bands, 0)
-    edge = jnp.zeros((chunks, size, rows, cols), jnp.bfloat16)
-    received[:, 0] = edge
-    received[:, n + 1] = edge
+    for chunk in range(chunks):
+        edge = jnp.zeros((sizes[chunk], rows, cols), jnp.bfloat16)
+        received[chunk][0] = edge
+        received[chunk][n + 1] = edge
 
     to_after.wait_recv()
     to_before.wait_recv()
@@ -282,11 +284,11 @@
         lax.fori_loop(1, n, await_strip, 0, unroll=flat_loop)
 
         def one(index, inner):
-            i = chunk * size + index
+            i = firsts[chunk] + index
             row_band = row_bands[i][:, : block + 2 * HALO]
             col_band = col_bands[i]
             for start in range(0, height, block):
-                window = received[chunk, pl.ds(start // rows, block // rows + 2), index]
+                window = received[chunk][pl.ds(start // rows, block // rows + 2), index]
                 window = window.reshape(block + 2 * rows, cols)[rows - HALO : rows + block + HALO]
                 moved = jnp.dot(row_band, window, preferred_element_type=jnp.float32)
                 moved = jnp.dot(
@@ -295,7 +297,7 @@
                 aligned_ref[i, pl.ds(start, block), :] = moved.astype(jnp.bfloat16)
             return inner
 
-        lax.fori_loop(0, size, one, 0, unroll=True)
+        lax.fori_loop(0, sizes[chunk], one, 0, unroll=min(4, sizes[chunk]))
 
     for own_copy in own_copies:
         own_copy.wait()
@@ -324,7 +326,7 @@
 
     def correlate(chunk):
         def pair(index, inner):
-            first = chunk * size + 2 * index
+            first = firsts[chunk] + 2 * index
             both = jnp.concatenate([aligned_ref[first], aligned_ref[first + 1]], axis=1)
             for a in range(WIDE):
                 products = jnp.dot(
@@ -345,7 +347,7 @@
                     diagonals[pl.ds(place, SUB), :] = total
             return inner
 
-        lax.fori_loop(0, size // 2, pair, 0)
+        lax.fori_loop(0, sizes[chunk] // 2, pair, 0)
 
     correlate(0)
 
@@ -397,11 +399,13 @@
     rows, cols, pixels = data.shape
     n = lax.axis_size("strip")
     part = pixels // n
-    chunks = max(1, part // 4)
+    quarter = part // 4
+    sizes = (part,) if part < 8 else (part - 2 * quarter, quarter, quarter)
+    chunks = len(sizes)
     height = n * rows
     block = min(128, height)
     reach = rows + 2 * HALO
-    assert rows >= HALO and rows % 16 == 0 and block % rows == 0 and (part // chunks) % 2 == 0 and height % block == 0
+    assert rows >= HALO and rows % 16 == 0 and block % rows == 0 and all(size % 2 == 0 for size in sizes) and height % block == 0
     scaling = 1.0 / math.sqrt(pixels * height * cols)
     span = TAPS + (-TAPS) % SUB
     vmem = pl.BlockSpec(memory_space=pltpu.VMEM)
@@ -413,7 +417,7 @@
         jax.ShapeDtypeStruct((part, WIDE * WIDE), f32),
     )
     results = pl.pallas_call(
-        functools.partial(kernel, n, chunks, scaling),
+        functools.partial(kernel, n, sizes, scaling),
         out_shape=shapes,
         in_specs=[hbm] * 4,
         out_specs=(vmem, vmem, vmem),
@@ -427,7 +431,7 @@
             pltpu.VMEM((pixels * rows, cols), f32),
             pltpu.VMEM((rows // 2, pixels, 2 * cols), bf16),
             pltpu.VMEM((pixels, rows, cols), bf16),
-            pltpu.VMEM((chunks, n + 2, part // chunks, rows, cols), bf16),
+            [pltpu.VMEM((n + 2, size, rows, cols), bf16) for size in sizes],
             pltpu.VMEM((part, block, 2 * block), bf16),
             pltpu.VMEM((part, cols, cols), bf16),
             pltpu.VMEM((part, 2 * block), jnp.int32),

time: 37.4 us -> 39.5 us (1.056)
  Pallas kernels: 36.6 us -> 38.7 us
    pallas_call x1, Pallas kernels: 35.6 us -> 37.7 us  [on_device(): pl.pallas_call(functools.partial(kernel, n, sizes, scaling), out_shape=sh...]
where the time goes in v8:
time: 39.5 us; the launch traced here: 39.3 us
  Pallas kernels  38.7 us (98%)
  between operations  0.64 us (2%)
    pallas_call x1, Pallas kernels, on_device(): pl.pallas_call(functools.partial(kernel, n, sizes, scaling), out_shape=sh...  37.7 us
    pallas_call x1, Pallas kernels, on_device(): pl.pallas_call(write_out, out_shape=shapes, in_specs=[vmem] * 3, out_spec...  1 us

profile of v8, /device:TPU:0, one launch (start us, length us, event | category | flops | bytes accessed | tf_op | source)
XLA Modules:
  0.0 39.3 jit_solution(1147293856339986624)
XLA Ops:
  0.6 37.7 %shard_map.67 = (bf16[16,256,128]{2,1,0:T(8,128)(2,1)S(1)}, f32[16,128]{1,0:T(8,128)S(1)}, f32[16,81]{1,0:T(8,128)S(1)}) custom-call(bf16[16,128,256]{2,1,0:T(8,128)(2,1)} %data_hbm.1, bf16[256,256]{1,0:T(8,128)(2,1)} %resp_hbm.1, s32[1,256]{1,0:T(1,128)} %bitcast.1, s32[2,256]{1,0:T(2,128)} %bins_hbm.1), custom_call_target="tpu_custom_call" | custom-call | tf_op jit(solution)/shard_map/pallas_call | solution.py:419
  38.3 1.0 %shard_map.68 = (bf16[16,256,128]{2,1,0:T(8,128)(2,1)}, f32[16,128]{1,0:T(8,128)}, f32[16,81]{1,0:T(8,128)}) custom-call(bf16[16,256,128]{2,1,0:T(8,128)(2,1)S(1)} %get-tuple-element.6.refs_0_, f32[16,128]{1,0:T(8,128)S(1)} %get-tuple-element.7.refs_1_, f32[16,81]{1,0:T(8,128)S(1)} %get-tuple-element.8.refs_2_), custom_call_target="tpu_custom_call" | custom-call | tf_op jit(solution)/shard_map/pallas_call | solution.py:464
